TPU v7x, 32 devices: a whole 2x2x4 slice. The times are simulated.
32 devices in a mesh: ctx: 8 (over z, y), head: 4 (over x, core).
Axes of the slice: x: 2, y: 2, z: 4, core: 2. Of those that a mesh axis runs over, the one named last changes fastest.
Arguments:
- conv_input: bfloat16 [6144, 8448], P(('ctx', 'head')), may hold values from -6 to 6
- conv_weight: float32 [4, 8448], replicated, may hold values from -3 to 3
- conv_bias: float32 [8448], replicated, may hold values from -3 to 3
- step_size: float32 [128, 6144], P('head', 'ctx'), may hold values from 0 to 0.12, as said below
- log_decay: float32 [128, 6144], P('head', 'ctx'), may hold values from -0.6 to 0, as said below
- skip_gain: float32 [128], P('head'), may hold values from 0.5 to 2
- grad_output: bfloat16 [6144, 8192], P('ctx', 'head'), may hold values from -6 to 6
Outputs:
- layer_output: bfloat16 [6144, 8192], P('ctx', 'head')
- grad_input: bfloat16 [6144, 8448], P(('ctx', 'head'))
- grad_step: float32 [128, 6144], P('head', 'ctx')
- grad_decay: float32 [128, 6144], P('head', 'ctx')
Inputs may be any that keep to these rules, and one draw needn't show every extreme that they name: `step_size`: positive step sizes. `log_decay`: negative logarithms of decays.
All inputs are finite; a program needn't handle non-finite values.
Results may differ from a plain program's by a relative error of at most 0.013.
Values may be sent and summed in bfloat16 or wider, within the bound.
A program may use at most 128 MiB of HBM per device.

v0:
```python
from functools import partial

import jax
import jax.numpy as jnp
from jax import lax
from jax.experimental import pallas as pl
from jax.experimental.pallas import tpu as pltpu
from jax.sharding import PartitionSpec as P

STATE = 128
BLOCK = 256
GROUP = 16
F32 = jnp.float32
BF16 = jnp.bfloat16
VMEM_LIMIT = 50 * 1024 * 1024


def dot(a, b, ca, cb):
    return lax.dot_general(
        a, b, (((ca,), (cb,)), ((), ())), preferred_element_type=F32
    )


def halves(value):
    high = value.astype(BF16)
    return high, (value - high.astype(F32)).astype(BF16)


def head_of_lane(rows, width, head_dim):
    row = lax.broadcasted_iota(jnp.int32, (rows, width), 0)
    lane = lax.broadcasted_iota(jnp.int32, (rows, width), 1)
    return jnp.where(lax.rem(row, GROUP) == lane // head_dim, 1.0, 0.0).astype(BF16)


def expand(rows, width, head_dim):
    high = rows.astype(BF16).astype(F32)
    both = jnp.concatenate([high, rows - high], axis=0).astype(BF16)
    return dot(both, head_of_lane(2 * GROUP, width, head_dim), 0, 0)


def head_sums(value, head_dim):
    pick = head_of_lane(GROUP, value.shape[1], head_dim)
    high, low = halves(value)
    return dot(pick, high, 1, 1) + dot(pick, low, 1, 1)


def earlier_or_same(length):
    row = lax.broadcasted_iota(jnp.int32, (length, length), 0)
    col = lax.broadcasted_iota(jnp.int32, (length, length), 1)
    return jnp.where(row <= col, 1.0, 0.0).astype(BF16)


def triangular(rows, contract):
    high = rows.astype(BF16).astype(F32)
    rest = rows - high
    middle = rest.astype(BF16).astype(F32)
    terms = jnp.concatenate([high, middle, rest - middle, jnp.zeros_like(rows)], axis=0)
    sums = dot(terms.astype(BF16), earlier_or_same(rows.shape[1]), 1, contract)
    return sums[:GROUP] + sums[GROUP : 2 * GROUP] + sums[2 * GROUP : 3 * GROUP]


def running_sum(rates):
    return triangular(rates, 0)


def states_kernel(head_dim, x_ref, m_ref, dy_ref, rate_ref, step_ref, inc_ref, gp_ref, dec_ref, pack_ref, t_ref, r_ref, d_ref):
    b = pl.program_id(1)
    width = x_ref.shape[1]
    cum = running_sum(rate_ref[...])
    last = cum[:, BLOCK - 1 :]
    to_end = expand(jnp.exp(last - cum) * step_ref[...], width, head_dim)
    from_start = expand(jnp.exp(cum), width, head_dim)
    xw = (x_ref[...].astype(F32) * to_end).astype(BF16)
    dyw = (dy_ref[...].astype(F32) * from_start).astype(BF16)
    inc = dot(m_ref[:, :STATE], xw, 0, 0)
    gp = dot(m_ref[:, STATE:], dyw, 0, 0)
    dec = from_start[BLOCK - 1 :]
    inc_ref[0] = inc
    gp_ref[0] = gp
    dec_ref[0] = jnp.broadcast_to(dec, (GROUP, width))

    @pl.when(b == 0)
    def _():
        t_ref[...] = inc
        r_ref[...] = gp
        d_ref[...] = jnp.broadcast_to(dec, d_ref.shape)

    @pl.when(b > 0)
    def _():
        t_ref[...] = t_ref[...] * dec + inc
        r_ref[...] = r_ref[...] + d_ref[0:1] * gp
        d_ref[...] = d_ref[...] * dec

    @pl.when(b == pl.num_programs(1) - 1)
    def _():
        decay = d_ref[...]
        high = decay.astype(BF16).astype(F32)
        both = jnp.concatenate([high, decay - high], axis=0).astype(BF16)
        pieces, rows, part = pack_ref.shape
        for i in range(pieces):
            lanes = slice(i * part, (i + 1) * part)
            pack_ref[i, :STATE] = t_ref[:, lanes].astype(BF16)
            pack_ref[i, STATE : 2 * STATE] = r_ref[:, lanes].astype(BF16)
            pack_ref[i, 2 * STATE :] = both[:, lanes]


def chain_kernel(in_ref, out_ref):
    peers, rows, part = in_ref.shape

    def decay(c):
        return in_ref[c, 2 * STATE : 2 * STATE + 1].astype(F32) + in_ref[
            c, 2 * STATE + GROUP : 2 * STATE + GROUP + 1
        ].astype(F32)

    state = jnp.zeros((STATE, part), F32)
    for c in range(peers):
        out_ref[c, :STATE] = state.astype(BF16)
        state = decay(c) * state + in_ref[c, :STATE].astype(F32)
    grad = jnp.zeros((STATE, part), F32)
    for c in range(peers - 1, -1, -1):
        out_ref[c, STATE:] = grad.astype(BF16)
        grad = decay(c) * grad + in_ref[c, STATE : 2 * STATE].astype(F32)


def intra_kernel(head_dim, x_ref, m_ref, dy_ref, rate_ref, step_ref, skip_ref, *refs):
    y_ref, dx_ref, gs_ref, gc_ref, gm_ref, aff_ref, da_ref = refs[-7:]
    g = pl.program_id(1)
    width = x_ref.shape[1]
    row = lax.broadcasted_iota(jnp.int32, (BLOCK, BLOCK), 0)
    col = lax.broadcasted_iota(jnp.int32, (BLOCK, BLOCK), 1)
    causal = row >= col

    @pl.when(g == 0)
    def _():
        aff_ref[...] = jnp.where(causal, dot(m_ref[:, STATE:], m_ref[:, :STATE], 1, 1), 0.0)
        da_ref[...] = jnp.zeros_like(da_ref)

    cum = running_sum(rate_ref[...])
    cum_col = cum.T
    x = x_ref[...].astype(F32)
    dy = dy_ref[...]
    steps = expand(step_ref[...], width, head_dim)
    xs = (x * steps).astype(BF16)
    pair = 2 * head_dim
    lane = lax.broadcasted_iota(jnp.int32, (BLOCK, pair), 1)
    ins_parts, back_parts = [], []
    for p in range(GROUP // 2):
        lanes = slice(p * pair, (p + 1) * pair)
        xs_p, dy_p = xs[:, lanes], dy[:, lanes]
        ins, back = 0.0, 0.0
        for k in range(2):
            h = 2 * p + k
            mine = (lane // head_dim) == k
            xs_h = jnp.where(mine, xs_p, jnp.zeros_like(xs_p))
            dy_h = jnp.where(mine, dy_p, jnp.zeros_like(dy_p))
            decay = jnp.exp(jnp.minimum(cum_col[:, h : h + 1] - cum[h : h + 1, :], 0.0))
            weights = (aff_ref[...] * decay).astype(BF16)
            ins = ins + dot(weights, xs_h, 1, 0)
            back = back + dot(weights, dy_h, 0, 0)
            da_ref[...] += dot(dy_h, xs_p, 1, 1) * decay
        ins_parts.append(ins)
        back_parts.append(back)
    ins = jnp.concatenate(ins_parts, axis=1)
    back = jnp.concatenate(back_parts, axis=1)
    skip = skip_ref[0:1]
    dyf = dy.astype(F32)
    y_ref[...] = (ins + skip * x).astype(BF16)
    dx_ref[...] = (steps * back + skip * dyf).astype(BF16)
    gs_ref[...] = head_sums(x * back, head_dim)
    gc_ref[...] = head_sums(dyf * ins, head_dim) - head_sums(xs.astype(F32) * back, head_dim)

    @pl.when(g == pl.num_programs(1) - 1)
    def _():
        da = jnp.where(causal, da_ref[...], 0.0).astype(BF16)
        gm_ref[:, :STATE] = dot(da, m_ref[:, STATE:], 0, 0)
        gm_ref[:, STATE:] = dot(da, m_ref[:, :STATE], 1, 0)


def carry_kernel(head_dim, x_ref, m_ref, dy_ref, rate_ref, step_ref, y1_ref, dx1_ref, gs1_ref, gc1_ref, gm1_ref,
                 inc_ref, gp_ref, dec_ref, enter_ref, *refs):
    y_ref, dx_ref, gs_ref, gd_ref, s_ref, g_ref, dot_ref, acc_ref = refs[-8:]
    b, g = pl.program_id(0), pl.program_id(1)
    width = x_ref.shape[1]
    blocks = inc_ref.shape[0]

    @pl.when(b == 0)
    def _():
        pieces = enter_ref.shape[0]
        state = jnp.concatenate([enter_ref[i, :STATE] for i in range(pieces)], axis=1).astype(F32)
        grad = jnp.concatenate([enter_ref[i, STATE:] for i in range(pieces)], axis=1).astype(F32)
        grads = [None] * blocks
        for k in range(blocks - 1, -1, -1):
            grads[k] = grad
            g_ref[k, g] = grad.astype(BF16)
            if k > 0:
                grad = dec_ref[k, 0:1] * grad + gp_ref[k]
        for k in range(blocks):
            s_ref[k, g] = state.astype(BF16)
            state = dec_ref[k, 0:1] * state + inc_ref[k]
            total = jnp.sum(state * grads[k], axis=0, keepdims=True)
            total = jnp.broadcast_to(total, (128, width))
            dot_ref[k, g] = head_sums(total, head_dim)

    cum = running_sum(rate_ref[...])
    ending = jnp.exp(cum[:, BLOCK - 1 :] - cum)
    weight = ending * step_ref[...]
    from_start = expand(jnp.exp(cum), width, head_dim)
    to_end = expand(weight, width, head_dim)
    x = x_ref[...].astype(F32)
    dy = dy_ref[...].astype(F32)
    state, grad = s_ref[b, g], g_ref[b, g]
    in_map, out_map = m_ref[:, :STATE], m_ref[:, STATE:]
    carried = from_start * dot(out_map, state, 1, 0)
    pulled = dot(in_map, grad, 1, 0)
    y_ref[...] = (y1_ref[...].astype(F32) + carried).astype(BF16)
    dx = (dx1_ref[...].astype(F32) + to_end * pulled).astype(BF16)
    lanes = pl.ds(pl.multiple_of(g * width, width), width)
    dx_ref[:, lanes] = dx
    xq = head_sums(x * pulled, head_dim)
    gs_ref[...] = gs1_ref[...] + ending * xq
    gc = gc1_ref[...] + head_sums(dy * carried, head_dim) - weight * xq
    at = lax.broadcasted_iota(jnp.int32, gc.shape, 1)
    gc = gc + jnp.where(at == BLOCK - 1, dot_ref[b, g][:, 0:1], 0.0)
    gd_ref[...] = triangular(gc, 1)
    d_in = dot((x * to_end).astype(BF16), grad, 1, 1)
    d_out = dot((dy * from_start).astype(BF16), state, 1, 1)

    @pl.when(g == 0)
    def _():
        acc_ref[...] = gm1_ref[...]
        for more_ref in refs[:-8]:
            acc_ref[...] += more_ref[...]

    acc_ref[:, :STATE] += d_in
    acc_ref[:, STATE:] += d_out

    @pl.when(g == pl.num_programs(1) - 1)
    def _():
        dx_ref[:, dx_ref.shape[1] - 2 * STATE :] = acc_ref[...].astype(BF16)


def params(order):
    return pltpu.CompilerParams(vmem_limit_bytes=VMEM_LIMIT, dimension_semantics=order)


def shifted(value, axis, by):
    peers = lax.axis_size(axis)
    pairs = [(i, i + by) for i in range(peers) if 0 <= i + by < peers]
    return lax.ppermute(value, axis, pairs)


def local(conv_input, conv_weight, conv_bias, step_size, log_decay, skip_gain, grad_output):
    taps_count = conv_weight.shape[0]
    tok_rows, channels = conv_input.shape
    heads_here, seq_rows = step_size.shape
    lanes = grad_output.shape[1]
    head_dim = lanes // heads_here
    peers = lax.axis_size("head")
    ctx = lax.axis_size("ctx")
    blocks = seq_rows // BLOCK
    groups = heads_here // GROUP
    width = GROUP * head_dim
    inner = peers * lanes
    full = lanes + 2 * STATE
    map_at = lanes // (2 * STATE)

    earlier = shifted(conv_input[tok_rows - (taps_count - 1) :], ("ctx", "head"), 1)
    padded = jnp.concatenate([earlier, conv_input], axis=0).astype(F32)
    preact = conv_bias[None, :] + conv_weight[0][None, :] * padded[0:tok_rows]
    for offset in range(1, taps_count):
        preact = preact + conv_weight[offset][None, :] * padded[offset : offset + tok_rows]
    activated, silu_back = jax.vjp(jax.nn.silu, preact)
    activated = activated.astype(BF16)
    maps = activated[:, inner:]
    send = jnp.concatenate(
        [
            jnp.concatenate([activated[:, i * lanes : (i + 1) * lanes], maps], axis=1)
            for i in range(peers)
        ],
        axis=0,
    )
    got = lax.all_to_all(send, "head", split_axis=0, concat_axis=0, tiled=True)

    part = lanes // ctx
    pieces = ctx // groups
    gb = [
        pl.BlockSpec((BLOCK, width), lambda g, b: (b, g)),
        pl.BlockSpec((BLOCK, 2 * STATE), lambda g, b: (b, map_at)),
        pl.BlockSpec((BLOCK, width), lambda g, b: (b, g)),
        pl.BlockSpec((GROUP, BLOCK), lambda g, b: (g, b)),
        pl.BlockSpec((GROUP, BLOCK), lambda g, b: (g, b)),
    ]
    bg = [
        pl.BlockSpec((BLOCK, width), lambda b, g: (b, g)),
        pl.BlockSpec((BLOCK, 2 * STATE), lambda b, g: (b, map_at)),
        pl.BlockSpec((BLOCK, width), lambda b, g: (b, g)),
        pl.BlockSpec((GROUP, BLOCK), lambda b, g: (g, b)),
        pl.BlockSpec((GROUP, BLOCK), lambda b, g: (g, b)),
    ]
    tile = pl.BlockSpec((BLOCK, width), lambda b, g: (b, g))
    rows = pl.BlockSpec((GROUP, BLOCK), lambda b, g: (g, b))
    mapgrad = pl.BlockSpec((BLOCK, 2 * STATE), lambda b, g: (b, 0))

    inc, gp, dec, packed = pl.pallas_call(
        partial(states_kernel, head_dim),
        grid=(groups, blocks),
        in_specs=gb,
        out_specs=[
            pl.BlockSpec((1, STATE, width), lambda g, b: (b, 0, g)),
            pl.BlockSpec((1, STATE, width), lambda g, b: (b, 0, g)),
            pl.BlockSpec((1, GROUP, width), lambda g, b: (b, 0, g)),
            pl.BlockSpec((pieces, 2 * STATE + 2 * GROUP, part), lambda g, b: (g, 0, 0)),
        ],
        out_shape=[
            jax.ShapeDtypeStruct((blocks, STATE, lanes), F32),
            jax.ShapeDtypeStruct((blocks, STATE, lanes), F32),
            jax.ShapeDtypeStruct((blocks, GROUP, lanes), F32),
            jax.ShapeDtypeStruct((ctx, 2 * STATE + 2 * GROUP, part), BF16),
        ],
        scratch_shapes=[
            pltpu.VMEM((STATE, width), F32),
            pltpu.VMEM((STATE, width), F32),
            pltpu.VMEM((GROUP, width), F32),
        ],
        compiler_params=params(("arbitrary", "arbitrary")),
        name="states",
    )(got, got, grad_output, log_decay, step_size)

    def columns(value):
        return lax.all_to_all(value, "ctx", split_axis=0, concat_axis=0, tiled=True)

    def chain(mine):
        return pl.pallas_call(
            chain_kernel,
            out_shape=jax.ShapeDtypeStruct((ctx, 2 * STATE, part), BF16),
            compiler_params=pltpu.CompilerParams(vmem_limit_bytes=VMEM_LIMIT),
            name="chain",
        )(mine)

    mine = columns(packed)

    skip = jnp.broadcast_to(jnp.repeat(skip_gain, head_dim)[None, :], (GROUP, lanes))
    SHARES = 2 if groups % 2 == 0 else 1
    share = groups // SHARES

    def intra(k, before):
        at = k * share
        wide = pl.BlockSpec((BLOCK, width), lambda b, g: (b, g + at))
        thin = pl.BlockSpec((GROUP, BLOCK), lambda b, g: (g + at, b))
        return pl.pallas_call(
            partial(intra_kernel, head_dim),
            grid=(blocks, share),
            in_specs=[
                wide,
                bg[1],
                wide,
                thin,
                thin,
                pl.BlockSpec((GROUP, width), lambda b, g: (0, g + at)),
            ]
            + [pl.BlockSpec(memory_space=pl.ANY)] * len(before),
            out_specs=[wide, wide, thin, thin, mapgrad],
            out_shape=[
                jax.ShapeDtypeStruct((seq_rows, lanes), BF16),
                jax.ShapeDtypeStruct((seq_rows, lanes), BF16),
                jax.ShapeDtypeStruct((heads_here, seq_rows), F32),
                jax.ShapeDtypeStruct((heads_here, seq_rows), F32),
                jax.ShapeDtypeStruct((seq_rows, 2 * STATE), F32),
            ],
            scratch_shapes=[pltpu.VMEM((BLOCK, BLOCK), F32), pltpu.VMEM((BLOCK, BLOCK), F32)],
            compiler_params=params(("arbitrary", "arbitrary")),
            cost_estimate=pl.CostEstimate(
                flops=10_000_000_000, bytes_accessed=50_000_000, transcendentals=3_000_000
            ),
            input_output_aliases={6 + i: i for i in range(len(before))},
            name="intra",
        )(got, got, grad_output, log_decay, step_size, skip, *before)

    *first, gm1 = intra(0, [])
    mine, first[2] = lax.optimization_barrier((mine, first[2]))
    entering = columns(chain(mine))
    gm2 = []
    if SHARES == 2:
        *first, more = intra(1, first)
        gm2 = [more]

    def once(*shape):
        return pl.BlockSpec(shape, lambda b, g: (0, 0, jnp.where(b == 0, g, groups - 1)))

    y, dx, grad_steps, grad_rates = pl.pallas_call(
        partial(carry_kernel, head_dim),
        grid=(blocks, groups),
        in_specs=bg
        + [
            tile,
            tile,
            rows,
            rows,
            mapgrad,
            once(blocks, STATE, width),
            once(blocks, STATE, width),
            once(blocks, GROUP, width),
            pl.BlockSpec((pieces, 2 * STATE, part), lambda b, g: (jnp.where(b == 0, g, groups - 1), 0, 0)),
        ]
        + [mapgrad] * len(gm2),
        out_specs=[tile, pl.BlockSpec((BLOCK, full), lambda b, g: (b, 0)), rows, rows],
        out_shape=[
            jax.ShapeDtypeStruct((seq_rows, lanes), BF16),
            jax.ShapeDtypeStruct((seq_rows, full), BF16),
            jax.ShapeDtypeStruct((heads_here, seq_rows), F32),
            jax.ShapeDtypeStruct((heads_here, seq_rows), F32),
        ],
        scratch_shapes=[
            pltpu.VMEM((blocks, groups, STATE, width), BF16),
            pltpu.VMEM((blocks, groups, STATE, width), BF16),
            pltpu.VMEM((blocks, groups, GROUP, 128), F32),
            pltpu.VMEM((BLOCK, 2 * STATE), F32),
        ],
        compiler_params=params(("arbitrary", "arbitrary")),
        name="carry",
    )(got, got, grad_output, log_decay, step_size, *first, gm1, inc, gp, dec, entering, *gm2)

    back = lax.all_to_all(dx, "head", split_axis=0, concat_axis=0, tiled=True)
    back = back.reshape(peers, tok_rows, full)
    map_grads = jnp.sum(back[:, :, lanes:].astype(F32), axis=0).astype(BF16)
    grad_act = jnp.concatenate([back[i, :, :lanes] for i in range(peers)] + [map_grads], axis=1)
    grad_pre = silu_back(grad_act.astype(F32))[0]
    following = shifted(grad_pre[: taps_count - 1], ("ctx", "head"), -1)
    extended = jnp.concatenate([grad_pre, following], axis=0)
    total = conv_weight[taps_count - 1][None, :] * extended[0:tok_rows]
    for offset in range(taps_count - 2, -1, -1):
        begin = taps_count - 1 - offset
        total = total + conv_weight[offset][None, :] * extended[begin : begin + tok_rows]
    return (y, total.astype(BF16), grad_steps, grad_rates)


def solution(mesh):
    return jax.shard_map(
        local,
        mesh=mesh,
        in_specs=(
            P(("ctx", "head"), None),
            P(),
            P(),
            P("head", "ctx"),
            P("head", "ctx"),
            P("head"),
            P("ctx", "head"),
        ),
        out_specs=(P("ctx", "head"), P(("ctx", "head"), None), P("head", "ctx"), P("head", "ctx")),
        check_vma=False,
    )
```

profile of v0, /device:TPU:9, one launch (start us, length us, event | category | flops | bytes accessed | tf_op | source)
XLA Modules:
  0.0 216.5 jit_solution(11832494455406368848)
XLA Ops:
  0.6 0.0 copy-start.12
  0.6 1.0 slice.73
  1.6 3.7 %collective-permute-start = (bf16[3,8448]{1,0:T(4,128)(2,1)S(1)}, bf16[3,8448]{1,0:T(4,128)(2,1)S(1)}, u32[]{:S(2)}, u32[]{:S(2)}) collective-permute-start(bf16[3,8448]{1,0:T(4,128)(2,1)S(1)} %slice.73), channel_id=1, source_target_pairs={{0,1},{1,2},{2,3},{3,4},{4,5},{5,6},{6,7},{7,8},{8,9},{9,10},{10,1... | collective-permute-start | bytes 152072 | tf_op jit(solution)/shard_map/ppermute | solution.py:249
  5.3 1.6 slice_reduce_fusion.4
  6.9 0.0 copy-start.8
  6.9 0.0 copy-start.10
  6.9 0.0 collective-permute-done
  6.9 2.6 %maximum_convert_fusion = f32[195,8448]{1,0:T(8,128)S(1)} fusion(bf16[192,8448]{1,0:T(8,128)(2,1)} %param.7, bf16[3,8448]{1,0:T(4,128)(2,1)S(1)} %collective-permute-done), kind=kLoop, calls=%fused_computation.30 | loop fusion | flops 6589440 | bytes 9884160 | tf_op jit(solution)/shard_map/convert_element_type | solution.py:268
  9.5 0.0 copy-done.12
  9.5 5.6 %multiply_convert_fusion = (bf16[192,8448]{1,0:T(8,128)(2,1)S(1)}, f32[192,8448]{1,0:T(8,128)}) fusion(f32[195,8448]{1,0:T(8,128)S(1)} %maximum_convert_fusion, f32[8448]{0:T(1024)S(1)} %get-tuple-element.46, f32[8448]{0:T(1024)S(1)} %get-tuple-element.47, f32[8448]{0:T(1024)S(1)} %get-tuple-element.45, f32[8448]{0:T(1024)S(1)} %get-tuple-element.44, ...), kind=kLoop, calls=%fused_computation.27 | loop fusion | flops 21086208 | bytes 35853312 | tf_op jit(solution)/shard_map/convert_element_type | solution.py:273
  15.1 0.0 copy-done.8
  15.1 0.0 copy-done.10
  15.1 0.1 concatenate.32
  15.2 0.3 fusion.20
  15.5 0.0 copy-start
  15.5 0.0 copy-start.1
  15.5 2.6 %pad_maximum_fusion.1 = bf16[768,2304]{1,0:T(8,128)(2,1)S(1)} fusion(bf16[192,2304]{1,0:T(8,128)(2,1)S(1)} %concatenate.32, bf16[192,256]{1,0:T(8,128)(2,1)S(1)} %slice.99, bf16[192,2048]{1,0:T(8,128)(2,1)S(1)} %get-tuple-element.51, bf16[192,2048]{1,0:T(8,128)(2,1)S(1)} %get-tuple-element.52, bf16[192,2048]{1,0:T(8,128)(2,1)S(1)} %get-tuple-element.50), kind=kLoop, calls=%fused_computation.29 | loop fusion | flops 24772608 | bytes 6881280 | tf_op jit(solution)/shard_map/concatenate | solution.py:275
  18.1 46.2 %all_to_all.30 = bf16[4,192,2304]{2,1,0:T(8,128)(2,1)} all-to-all(bf16[4,192,2304]{2,1,0:T(8,128)(2,1)S(1)} %bitcast.29), channel_id=1, replica_groups=mesh['ctx'=8,'head'=4] {'head'}, dimensions={0} | all-to-all | bytes 7077888 | tf_op jit(solution)/shard_map/all_to_all | solution.py:282
  64.3 0.0 copy-done
  64.3 10.0 %states.1 = (f32[3,128,2048]{2,1,0:T(8,128)}, f32[3,128,2048]{2,1,0:T(8,128)}, f32[3,16,2048]{2,1,0:T(8,128)S(1)}, bf16[8,288,256]{2,1,0:T(8,128)(2,1)}) custom-call(bf16[768,2304]{1,0:T(8,128)(2,1)} %bitcast.19, bf16[768,2304]{1,0:T(8,128)(2,1)} %bitcast.20, bf16[768,2048]{1,0:T(8,128)(2,1)} %dy_ref.7, f32[32,768]{1,0:T(8,128)S(1)} %copy-done, ...), custom_call_target="tpu_custom_call" | custom-call | tf_op jit(solution)/shard_map/states/pallas_call | solution.py:304
  74.3 4.8 %all-to-all-start.1 = ((bf16[8,288,256]{2,1,0:T(8,128)(2,1)}), bf16[8,288,256]{2,1,0:T(8,128)(2,1)S(1)}, u32[]{:S(2)}, u32[]{:S(2)}) async-start(bf16[8,288,256]{2,1,0:T(8,128)(2,1)} %get-tuple-element.26), calls=%async_computation.1 | async-start | bytes 2359296 | tf_op jit(solution)/shard_map/all_to_all | solution.py:330
  79.1 0.1 broadcast_in_dim.11
  79.2 0.1 broadcast_in_dim.12
  79.3 14.2 %intra.2 = (bf16[768,2048]{1,0:T(8,128)(2,1)}, bf16[768,2048]{1,0:T(8,128)(2,1)}, f32[32,768]{1,0:T(8,128)S(1)}, f32[32,768]{1,0:T(8,128)S(1)}, f32[768,256]{1,0:T(8,128)S(1)}) custom-call(bf16[768,2304]{1,0:T(8,128)(2,1)} %bitcast.21, bf16[768,2304]{1,0:T(8,128)(2,1)} %bitcast.22, bf16[768,2048]{1,0:T(8,128)(2,1)} %dy_ref.7, f32[32,768]{1,0:T(8,128)S(1)} %copy-done, ...), custom_call_target="tpu_custom_call" | custom-call | flops 10000000000 | bytes 50000000 | tf_op jit(solution)/shard_map/intra/pallas_call | solution.py:350
  93.5 0.6 copy-done.2
  94.2 10.5 %all-to-all-done.1.in_ref = bf16[8,288,256]{2,1,0:T(8,128)(2,1)S(1)} async-done(((bf16[8,288,256]{2,1,0:T(8,128)(2,1)}), bf16[8,288,256]{2,1,0:T(8,128)(2,1)S(1)}, u32[]{:S(2)}, u32[]{:S(2)}) %all-to-all-start.1) | async-done | bytes 1179680 | tf_op jit(solution)/shard_map/all_to_all | solution.py:330
  104.7 1.2 chain.1
  105.9 6.8 %all-to-all-start.2 = ((bf16[8,256,256]{2,1,0:T(8,128)(2,1)}), bf16[8,256,256]{2,1,0:T(8,128)(2,1)S(1)}, u32[]{:S(2)}, u32[]{:S(2)}) async-start(bf16[8,256,256]{2,1,0:T(8,128)(2,1)} %chain.1), calls=%async_computation.2 | async-start | bytes 2097152 | tf_op jit(solution)/shard_map/all_to_all | solution.py:330
  112.7 0.9 copy-done.3
  113.6 0.9 copy-done.5
  114.5 14.2 %intra.3 = (bf16[768,2048]{1,0:T(8,128)(2,1)}, bf16[768,2048]{1,0:T(8,128)(2,1)}, f32[32,768]{1,0:T(8,128)S(1)}, f32[32,768]{1,0:T(8,128)S(1)}, f32[768,256]{1,0:T(8,128)S(1)}) custom-call(bf16[768,2304]{1,0:T(8,128)(2,1)} %bitcast.23, bf16[768,2304]{1,0:T(8,128)(2,1)} %bitcast.24, ...), custom_call_target="tpu_custom_call", output_to_operand_aliasing={{0}: (6, {}), {1}: (7, {}), {2}: (8, {}), {3}: (9, {})} | custom-call | flops 10000000000 | bytes 50000000 | tf_op jit(solution)/shard_map/intra/pallas_call | solution.py:350
  128.7 0.6 copy-done.6
  129.3 6.3 %all-to-all-done.2.enter_ref = bf16[8,256,256]{2,1,0:T(8,128)(2,1)S(1)} async-done(((bf16[8,256,256]{2,1,0:T(8,128)(2,1)}), bf16[8,256,256]{2,1,0:T(8,128)(2,1)S(1)}, u32[]{:S(2)}, u32[]{:S(2)}) %all-to-all-start.2) | async-done | bytes 1048608 | tf_op jit(solution)/shard_map/all_to_all | solution.py:330
  135.6 0.9 copy-done.7
  136.5 20.2 %carry.1 = (bf16[768,2048]{1,0:T(8,128)(2,1)}, bf16[768,2304]{1,0:T(8,128)(2,1)}, f32[32,768]{1,0:T(8,128)}, f32[32,768]{1,0:T(8,128)}) custom-call(bf16[768,2304]{1,0:T(8,128)(2,1)} %bitcast.25, bf16[768,2304]{1,0:T(8,128)(2,1)} %bitcast.26, bf16[768,2048]{1,0:T(8,128)(2,1)} %dy_ref.7, f32[32,768]{1,0:T(8,128)S(1)} %copy-done, f32[32,768]{1,0:T(8,128)S(1)} %copy-done.1, ...), custom_call_target="tpu_custom_call" | custom-call | tf_op jit(solution)/shard_map/carry/pallas_call | solution.py:390
  156.7 0.0 slice-start
  156.7 0.0 slice-start.1
  156.7 45.9 %all_to_all.31 = bf16[4,192,2304]{2,1,0:T(8,128)(2,1)S(1)} all-to-all(bf16[4,192,2304]{2,1,0:T(8,128)(2,1)} %bitcast.30), channel_id=1, replica_groups=mesh['ctx'=8,'head'=4] {'head'}, dimensions={0} | all-to-all | bytes 7077888 | tf_op jit(solution)/shard_map/all_to_all | solution.py:423
  202.6 0.1 slice_reduce_fusion
  202.7 0.1 fusion.18
  202.7 0.1 fusion.17
  202.8 0.1 fusion.16
  202.9 0.1 fusion.15
  203.0 2.4 %fusion.8 = f32[192,8448]{1,0:T(8,128)S(1)} fusion(bf16[192,8448]{1,0:T(8,128)(2,1)S(1)} %constant_dynamic-update-slice_fusion, f32[192,8448]{1,0:T(8,128)S(1)} %bitcast.28), kind=kLoop, calls=%fused_computation.15 | loop fusion | flops 16220160 | bytes 16220160 | tf_op jit(solution)/shard_map/transpose(jvp(jit(silu)))/add_any | solution.py:272
  205.4 2.9 %collective-permute-start.1 = (f32[3,8448]{1,0:T(4,128)S(1)}, f32[3,8448]{1,0:T(4,128)S(1)}, u32[]{:S(2)}, u32[]{:S(2)}) collective-permute-start(f32[3,8448]{1,0:T(4,128)S(1)} %slice.107), channel_id=1, source_target_pairs={{1,0},{2,1},{3,2},{4,3},{5,4},{6,5},{7,6},{8,7},{9,8},{10,9},{11,1... | collective-permute-start | bytes 304136 | tf_op jit(solution)/shard_map/ppermute | solution.py:249
  208.4 3.4 %collective-permute-done.1 = f32[3,8448]{1,0:T(4,128)S(1)} collective-permute-done((f32[3,8448]{1,0:T(4,128)S(1)}, f32[3,8448]{1,0:T(4,128)S(1)}, u32[]{:S(2)}, u32[]{:S(2)}) %collective-permute-start.1) | collective-permute-done | bytes 101408 | tf_op jit(solution)/shard_map/ppermute | solution.py:249
  211.8 0.0 copy-done.11
  211.8 4.7 %fusion.4 = bf16[192,8448]{1,0:T(8,128)(2,1)} fusion(f32[192,8448]{1,0:T(8,128)S(1)} %fusion.8, f32[3,8448]{1,0:T(4,128)S(1)} %collective-permute-done.1, f32[8448]{0:T(1024)S(1)} %copy-done.9, f32[8448]{0:T(1024)S(1)} %copy-done.11, f32[8448]{0:T(1024)S(1)} %get-tuple-element.45, f32[8448]{0:T(1024)S(1)} %get-tuple-element.44), kind=kLoop, calls=%fused_computation.11 | loop fusion | flops 17842176 | bytes 9968640 | tf_op jit(solution)/shard_map/convert_element_type | solution.py:434
  (20 shorter events, 0.1 us)
Async XLA Ops:
  0.6 8.9 %copy-start.12 = (f32[8448]{0:T(1024)S(1)}, f32[8448]{0:T(1024)}, u32[]{:S(2)}) copy-start(f32[8448]{0:T(1024)} %param.9) | copy-start | bytes 101380
  1.6 5.3 %collective-permute-start = (bf16[3,8448]{1,0:T(4,128)(2,1)S(1)}, bf16[3,8448]{1,0:T(4,128)(2,1)S(1)}, u32[]{:S(2)}, u32[]{:S(2)}) collective-permute-start(bf16[3,8448]{1,0:T(4,128)(2,1)S(1)} %slice.73), channel_id=1, source_target_pairs={{0,1},{1,2},{2,3},{3,4},{4,5},{5,6},{6,7},{7,8},{8,9},{9,10},{10,1... | collective-permute-start | bytes 152072 | tf_op jit(solution)/shard_map/ppermute | solution.py:249
  6.9 8.2 %copy-start.8 = (f32[8448]{0:T(1024)}, f32[8448]{0:T(1024)S(1)}, u32[]{:S(2)}) copy-start(f32[8448]{0:T(1024)S(1)} %get-tuple-element.46) | copy-start | bytes 101380
  6.9 8.2 %copy-start.10 = (f32[8448]{0:T(1024)}, f32[8448]{0:T(1024)S(1)}, u32[]{:S(2)}) copy-start(f32[8448]{0:T(1024)S(1)} %get-tuple-element.47) | copy-start | bytes 101380
  15.5 48.8 %copy-start = (f32[32,768]{1,0:T(8,128)S(1)}, f32[32,768]{1,0:T(8,128)}, u32[]{:S(2)}) copy-start(f32[32,768]{1,0:T(8,128)} %rate_ref.7) | copy-start | bytes 294916
  15.5 48.8 %copy-start.1 = (f32[32,768]{1,0:T(8,128)S(1)}, f32[32,768]{1,0:T(8,128)}, u32[]{:S(2)}) copy-start(f32[32,768]{1,0:T(8,128)} %step_ref.7) | copy-start | bytes 294916
  64.3 14.8 %copy-start.13 = (f32[32]{0:T(128)S(1)}, f32[32]{0:T(128)}, u32[]{:S(2)}) copy-start(f32[32]{0:T(128)} %param.12) | copy-start | bytes 388
  74.3 30.4 %all-to-all-start.1 = ((bf16[8,288,256]{2,1,0:T(8,128)(2,1)}), bf16[8,288,256]{2,1,0:T(8,128)(2,1)S(1)}, u32[]{:S(2)}, u32[]{:S(2)}) async-start(bf16[8,288,256]{2,1,0:T(8,128)(2,1)} %get-tuple-element.26), calls=%async_computation.1 | async-start | bytes 2359296 | tf_op jit(solution)/shard_map/all_to_all | solution.py:330
  93.5 0.6 copy-start.2
  94.2 18.5 %copy-start.4 = (f32[32,768]{1,0:T(8,128)}, f32[32,768]{1,0:T(8,128)S(1)}, u32[]{:S(2)}) copy-start(f32[32,768]{1,0:T(8,128)S(1)} %get-tuple-element.29.refs_3_) | copy-start | bytes 294916
  105.9 29.7 %all-to-all-start.2 = ((bf16[8,256,256]{2,1,0:T(8,128)(2,1)}), bf16[8,256,256]{2,1,0:T(8,128)(2,1)S(1)}, u32[]{:S(2)}, u32[]{:S(2)}) async-start(bf16[8,256,256]{2,1,0:T(8,128)(2,1)} %chain.1), calls=%async_computation.2 | async-start | bytes 2097152 | tf_op jit(solution)/shard_map/all_to_all | solution.py:330
  112.7 0.9 copy-start.3
  113.6 0.9 copy-start.5
  128.7 0.6 copy-start.6
  135.6 0.9 copy-start.7
  156.7 46.2 %slice-start = ((s8[6488064]{0:T(1024)(128)(4,1)}), s8[4194304]{0:T(1024)(128)(4,1)S(1)}, s32[]{:S(2)}) async-start(s8[6488064]{0:T(1024)(128)(4,1)} %bitcast.27), calls=%async_computation.4 | async-start | bytes 8388608
  156.7 46.2 %slice-start.1 = ((s8[6488064]{0:T(1024)(128)(4,1)}), s8[2293760]{0:T(1024)(128)(4,1)S(1)}, s32[]{:S(2)}) async-start(s8[6488064]{0:T(1024)(128)(4,1)} %bitcast.27), calls=%async_computation.5 | async-start | bytes 4587520
  203.0 8.8 %copy-start.9 = (f32[8448]{0:T(1024)S(1)}, f32[8448]{0:T(1024)}, u32[]{:S(2)}) copy-start(f32[8448]{0:T(1024)} %copy-done.8) | copy-start | bytes 101380
  203.0 8.8 %copy-start.11 = (f32[8448]{0:T(1024)S(1)}, f32[8448]{0:T(1024)}, u32[]{:S(2)}) copy-start(f32[8448]{0:T(1024)} %copy-done.10) | copy-start | bytes 101380
  205.4 6.3 %collective-permute-start.1 = (f32[3,8448]{1,0:T(4,128)S(1)}, f32[3,8448]{1,0:T(4,128)S(1)}, u32[]{:S(2)}, u32[]{:S(2)}) collective-permute-start(f32[3,8448]{1,0:T(4,128)S(1)} %slice.107), channel_id=1, source_target_pairs={{1,0},{2,1},{3,2},{4,3},{5,4},{6,5},{7,6},{8,7},{9,8},{10,9},{11,1... | collective-permute-start | bytes 304136 | tf_op jit(solution)/shard_map/ppermute | solution.py:249
where the time goes:
time: 220 us; the launch traced here: 216 us
  blocking collectives  92.1 us (42%)
  Pallas kernels  59.8 us (27%)
  waiting for transfers between devices  20.2 us (9%)
  starting transfers between devices  18.2 us (8%)
  other arithmetic  17.9 us (8%)
  local copies, waits for them, and re-layouts  7.32 us (3%)
    all_to_all x1, blocking collectives, local(): got = lax.all_to_all(send, 'head', split_axis=0, concat_axis=0, tiled=True)  46.2 us
    all_to_all x1, blocking collectives, local(): back = lax.all_to_all(dx, 'head', split_axis=0, concat_axis=0, tiled=True)  45.9 us
    pallas_call x2, Pallas kernels, intra(): pl.pallas_call(partial(intra_kernel, head_dim), grid=(blocks, share), in_...  28.5 us
    pallas_call x1, Pallas kernels, local(): pl.pallas_call(partial(carry_kernel, head_dim), grid=(blocks, groups), in...  20.2 us
    all_to_all x2, waiting for transfers between devices, columns(): return lax.all_to_all(value, 'ctx', split_axis=0, concat_axis=0, tiled=True)  16.8 us
    all_to_all x2, starting transfers between devices, columns(): return lax.all_to_all(value, 'ctx', split_axis=0, concat_axis=0, tiled=True)  11.6 us
    pallas_call x1, Pallas kernels, local(): pl.pallas_call(partial(states_kernel, head_dim), grid=(groups, blocks), i...  9.99 us
    ppermute x2, starting transfers between devices, shifted(): return lax.ppermute(value, axis, pairs)  6.63 us
  transfers between devices with their start and end apart: 4, of which 3 were waited for; matrix products, arithmetic and copies ran while one was open for 1% of the time, Pallas kernels for 13%

commit v1 on v0

v1 whole, which is shorter than its diff:
```python
from functools import partial

import jax
import jax.numpy as jnp
from jax import lax
from jax.experimental import pallas as pl
from jax.experimental.pallas import tpu as pltpu
from jax.sharding import PartitionSpec as P

STATE = 128
BLOCK = 256
GROUP = 8
TILE = 128
F32 = jnp.float32
BF16 = jnp.bfloat16
VMEM_LIMIT = 60 * 1024 * 1024
MESH = pl.DeviceIdType.MESH


def dot(a, b, ca, cb):
    return lax.dot_general(
        a, b, (((ca,), (cb,)), ((), ())), preferred_element_type=F32
    )


def head_of_lane(rows, width, head_dim):
    row = lax.broadcasted_iota(jnp.int32, (rows, width), 0)
    lane = lax.broadcasted_iota(jnp.int32, (rows, width), 1)
    return jnp.where(lax.rem(row, GROUP) == lane // head_dim, 1.0, 0.0).astype(BF16)


def expand(rows, width, head_dim):
    high = rows.astype(BF16).astype(F32)
    both = jnp.concatenate([high, rows - high], axis=0).astype(BF16)
    return dot(both, head_of_lane(2 * GROUP, width, head_dim), 0, 0)


def head_sums(value, head_dim):
    pick = head_of_lane(2 * GROUP, value.shape[1], head_dim)
    high = value.astype(BF16)
    low = (value - high.astype(F32)).astype(BF16)
    return (dot(pick, high, 1, 1) + dot(pick, low, 1, 1))[:GROUP]


def triangular(rows, contract):
    length = rows.shape[1]
    row = lax.broadcasted_iota(jnp.int32, (length, length), 0)
    col = lax.broadcasted_iota(jnp.int32, (length, length), 1)
    upper = jnp.where(row <= col, 1.0, 0.0).astype(BF16)
    high = rows.astype(BF16).astype(F32)
    rest = rows - high
    middle = rest.astype(BF16).astype(F32)
    terms = jnp.concatenate([high, middle, rest - middle, jnp.zeros_like(rows)], axis=0)
    sums = dot(terms.astype(BF16), upper, 1, contract)
    return sums[:GROUP] + sums[GROUP : 2 * GROUP] + sums[2 * GROUP : 3 * GROUP]


def at(start, size):
    return pl.ds(pl.multiple_of(start, size), size)


def mixer_kernel(
    H, C, head_dim,
    cin, cw, cb, step, rate, skip, dy,
    y, gin, gs, gd,
    halo, act, actm, dsil, xbuf, mbuf, cums, aff, da, inc, gp, dec,
    t_ref, r_ref, d_ref, tsend, inbox, outbox, ent, s_ref, g_ref, dots,
    gs1, gc1, dxbuf, rbuf, acc, gms, gmr, hsend, hrecv,
    halo_sem, x_send, x_recv, m_send, m_recv, t_send, t_recv, e_send, e_recv,
    b_send, b_recv, g_send, g_recv, h_send, h_recv,
):
    taps = cw.shape[0]
    TR, channels = cin.shape
    SR, lanes = dy.shape
    K, _, W = xbuf.shape
    NB = SR // BLOCK
    TPC = W // TILE
    inner = H * lanes
    c = lax.axis_index("ctx")
    head = lax.axis_index("head")
    index = c * H + head
    total = C * H
    order = sorted(range(1, H), key=lambda o: abs(o - H // 2))

    def where_is(i):
        return (i // H, i % H)

    following = where_is((index + 1) % total)
    preceding = where_is((index + total - 1) % total)

    barrier = pltpu.get_barrier_semaphore()
    for o in range(1, H):
        pl.semaphore_signal(barrier, inc=1, device_id=(c, (head + o) % H), device_id_type=MESH)
    for o in range(1, C):
        pl.semaphore_signal(barrier, inc=1, device_id=((c + o) % C, head), device_id_type=MESH)
    for who in (following, preceding):
        pl.semaphore_signal(barrier, inc=1, device_id=who, device_id_type=MESH)
    pl.semaphore_wait(barrier, H + C)

    def remote(src, dst, send, recv, who):
        return pltpu.make_async_remote_copy(
            src_ref=src, dst_ref=dst, send_sem=send, recv_sem=recv, device_id=who, device_id_type=MESH
        )

    halo_copy = remote(cin.at[pl.ds(TR - 16, 16)], halo, halo_sem.at[0], halo_sem.at[1], following)

    @pl.when(index < total - 1)
    def _():
        halo_copy.start()

    @pl.when(index > 0)
    def _():
        halo_copy.wait_recv()

    @pl.when(index == 0)
    def _():
        halo[...] = jnp.zeros_like(halo)

    def convolve(col):
        where = at(col, TILE)
        body = cin[:, where].astype(F32)
        padded = jnp.concatenate([halo[:, where].astype(F32)[8:], body], axis=0)
        first = 8 - (taps - 1)
        pre = cb[:, where] + cw[0:1, where] * padded[first : first + TR]
        for tap in range(1, taps):
            pre = pre + cw[tap : tap + 1, where] * padded[first + tap : first + tap + TR]
        sig = 0.5 * jnp.tanh(0.5 * pre) + 0.5
        value = pre * sig
        dsil[:, where] = (sig + value * (1.0 - sig)).astype(BF16)
        return value.astype(BF16)

    def peer(o):
        return (head + o) % H

    def source(o):
        return (head + H - o) % H

    def send_maps(o):
        return remote(actm, mbuf.at[at(head * TR, TR)], m_send.at[o], m_recv.at[o], (c, peer(o)))

    def recv_maps(o):
        return remote(actm, mbuf.at[at(source(o) * TR, TR)], m_send.at[o], m_recv.at[o], (c, peer(o)))

    def send_x(k, o):
        return remote(
            act.at[k, peer(o)], xbuf.at[k, at(head * TR, TR)], x_send.at[k, o], x_recv.at[k, o], (c, peer(o))
        )

    def recv_x(k, o):
        return remote(
            act.at[k, peer(o)], xbuf.at[k, at(source(o) * TR, TR)], x_send.at[k, o], x_recv.at[k, o], (c, peer(o))
        )

    for i in range(2 * STATE // TILE):
        actm[:, i * TILE : (i + 1) * TILE] = convolve(inner + i * TILE)
    for o in order:
        send_maps(o).start()
    mbuf[at(head * TR, TR), :] = actm[...]

    def conv_chunk(k, carry):
        for o in order + [0]:
            p = peer(o)
            for i in range(TPC):
                value = convolve(p * lanes + k * W + i * TILE)
                if o:
                    act[k, p, :, i * TILE : (i + 1) * TILE] = value
                else:
                    xbuf[k, at(head * TR, TR), i * TILE : (i + 1) * TILE] = value
            if o:
                send_x(k, o).start()
        return carry

    lax.fori_loop(0, K, conv_chunk, 0)

    def sums_chunk(k, carry):
        for b in range(NB):
            cums[k, b] = triangular(rate[at(k * GROUP, GROUP), b * BLOCK : (b + 1) * BLOCK], 0)
        return carry

    lax.fori_loop(0, K, sums_chunk, 0)

    for o in order:
        recv_maps(o).wait_recv()

    row = lax.broadcasted_iota(jnp.int32, (BLOCK, BLOCK), 0)
    col = lax.broadcasted_iota(jnp.int32, (BLOCK, BLOCK), 1)
    causal = row >= col
    for b in range(NB):
        m = mbuf[b * BLOCK : (b + 1) * BLOCK]
        aff[b] = jnp.where(causal, dot(m[:, STATE:], m[:, :STATE], 1, 1), 0.0)
        da[b] = jnp.zeros((BLOCK, BLOCK), F32)
    acc[...] = jnp.zeros_like(acc)

    def owner(k, j):
        return (k * TPC + j) % C

    def send_tile(k, j):
        return remote(tsend.at[k, j], inbox.at[k, c], t_send.at[k, j], t_recv.at[k, c], (owner(k, j), head))

    def recv_tile(k, src):
        return remote(tsend.at[k, 0], inbox.at[k, src], t_send.at[k, 0], t_recv.at[k, src], (src, head))

    def states(k):
        t_ref[...] = jnp.zeros_like(t_ref)
        r_ref[...] = jnp.zeros_like(r_ref)
        d_ref[...] = jnp.ones_like(d_ref)

        def block(b, carry):
            rows = at(b * BLOCK, BLOCK)
            x = xbuf[k, rows, :]
            cum = cums[k, b]
            last = cum[:, BLOCK - 1 :]
            to_end = expand(jnp.exp(last - cum) * step[at(k * GROUP, GROUP), rows], W, head_dim)
            from_start = expand(jnp.exp(cum), W, head_dim)
            xw = (x.astype(F32) * to_end).astype(BF16)
            dyw = (dy[rows, at(k * W, W)].astype(F32) * from_start).astype(BF16)
            more = dot(mbuf[rows, :STATE], xw, 0, 0)
            grad = dot(mbuf[rows, STATE:], dyw, 0, 0)
            last_dec = from_start[BLOCK - 1 :]
            inc[k, b] = more
            gp[k, b] = grad
            dec[k, b] = jnp.broadcast_to(last_dec, (GROUP, W))
            t_ref[...] = t_ref[...] * last_dec + more
            r_ref[...] = r_ref[...] + d_ref[0:1] * grad
            d_ref[...] = d_ref[...] * last_dec
            return carry

        lax.fori_loop(0, NB, block, 0)
        decay = d_ref[...]
        high = decay.astype(BF16).astype(F32)
        both = jnp.concatenate([high, decay - high], axis=0).astype(BF16)
        for j in range(TPC):
            where = slice(j * TILE, (j + 1) * TILE)
            tsend[k, j, :STATE] = t_ref[:, where].astype(BF16)
            tsend[k, j, STATE : 2 * STATE] = r_ref[:, where].astype(BF16)
            tsend[k, j, 2 * STATE :] = both[:, where]

        for j in range(TPC):
            @pl.when(owner(k, j) == c)
            def _():
                inbox[k, c] = tsend[k, j]

            @pl.when(owner(k, j) != c)
            def _():
                send_tile(k, j).start()

    def send_enter(k, j, dst):
        return remote(outbox.at[k, dst], ent.at[k, j], e_send.at[k, dst], e_recv.at[k, j], (dst, head))

    def chain(k):
        j = (c + total * TPC - k * TPC) % C

        @pl.when(j < TPC)
        def _():
            def arrive(src, carry):
                @pl.when(src != c)
                def _():
                    recv_tile(k, src).wait_recv()
                return carry

            lax.fori_loop(0, C, arrive, 0)

            def decay(src):
                both = inbox[k, src, 2 * STATE :].astype(F32)
                return both[0:1] + both[GROUP : GROUP + 1]

            def ahead(i, state):
                outbox[k, i, :STATE] = state.astype(BF16)
                return decay(i) * state + inbox[k, i, :STATE].astype(F32)

            def astern(i, grad):
                i = C - 1 - i
                outbox[k, i, STATE:] = grad.astype(BF16)
                return decay(i) * grad + inbox[k, i, STATE : 2 * STATE].astype(F32)

            lax.fori_loop(0, C, ahead, jnp.zeros((STATE, TILE), F32))
            lax.fori_loop(0, C, astern, jnp.zeros((STATE, TILE), F32))

            def leave(dst, carry):
                @pl.when(dst != c)
                def _():
                    send_enter(k, j, dst).start()
                return carry

            lax.fori_loop(0, C, leave, 0)
            ent[k, j] = outbox[k, c]

    def intra(k):
        pair = 2 * head_dim
        lane = lax.broadcasted_iota(jnp.int32, (BLOCK, pair), 1)

        def block(b, carry):
            rows = at(b * BLOCK, BLOCK)
            heads = at(k * GROUP, GROUP)
            wide = at(k * W, W)
            cum = cums[k, b]
            cum_col = cum.T
            x = xbuf[k, rows, :].astype(F32)
            dyb = dy[rows, wide]
            steps = expand(step[heads, rows], W, head_dim)
            xs = (x * steps).astype(BF16)
            ins_parts, back_parts = [], []
            for p in range(GROUP // 2):
                part = slice(p * pair, (p + 1) * pair)
                xs_p, dy_p = xs[:, part], dyb[:, part]
                ins, back = 0.0, 0.0
                for side in range(2):
                    h = 2 * p + side
                    mine = (lane // head_dim) == side
                    xs_h = jnp.where(mine, xs_p, jnp.zeros_like(xs_p))
                    dy_h = jnp.where(mine, dy_p, jnp.zeros_like(dy_p))
                    decay = jnp.exp(jnp.minimum(cum_col[:, h : h + 1] - cum[h : h + 1, :], 0.0))
                    weights = (aff[b] * decay).astype(BF16)
                    ins = ins + dot(weights, xs_h, 1, 0)
                    back = back + dot(weights, dy_h, 0, 0)
                    da[b] += dot(dy_h, xs_p, 1, 1) * decay
                ins_parts.append(ins)
                back_parts.append(back)
            ins = jnp.concatenate(ins_parts, axis=1)
            back = jnp.concatenate(back_parts, axis=1)
            gain = skip[0:1, wide]
            dyf = dyb.astype(F32)
            y[rows, wide] = (ins + gain * x).astype(BF16)
            dxbuf[k, rows, :] = (steps * back + gain * dyf).astype(BF16)
            gs1[k, b] = head_sums(x * back, head_dim)
            gc1[k, b] = head_sums(dyf * ins - xs.astype(F32) * back, head_dim)
            return carry

        lax.fori_loop(0, NB, block, 0)

    def send_back(k, o):
        return remote(
            dxbuf.at[k, at(peer(o) * TR, TR)], rbuf.at[k, head], b_send.at[k, o], b_recv.at[k, o], (c, peer(o))
        )

    def recv_back(k, o):
        return remote(
            dxbuf.at[k, at(peer(o) * TR, TR)], rbuf.at[k, source(o)], b_send.at[k, o], b_recv.at[k, o], (c, peer(o))
        )

    def carry_over(k):
        for j in range(TPC):
            @pl.when(owner(k, j) != c)
            def _():
                remote(
                    outbox.at[k, 0], ent.at[k, j], e_send.at[k, 0], e_recv.at[k, j], (owner(k, j), head)
                ).wait_recv()

        state = jnp.concatenate([ent[k, j, :STATE] for j in range(TPC)], axis=1).astype(F32)
        grad = jnp.concatenate([ent[k, j, STATE:] for j in range(TPC)], axis=1).astype(F32)
        grads = [None] * NB
        for b in range(NB - 1, -1, -1):
            grads[b] = grad
            g_ref[b] = grad.astype(BF16)
            if b > 0:
                grad = dec[k, b, 0:1] * grad + gp[k, b]
        for b in range(NB):
            s_ref[b] = state.astype(BF16)
            state = dec[k, b, 0:1] * state + inc[k, b]
            both = jnp.sum(state * grads[b], axis=0, keepdims=True)
            dots[b] = head_sums(jnp.broadcast_to(both, (TILE, W)), head_dim)

        def block(b, carry):
            rows = at(b * BLOCK, BLOCK)
            heads = at(k * GROUP, GROUP)
            wide = at(k * W, W)
            cum = cums[k, b]
            ending = jnp.exp(cum[:, BLOCK - 1 :] - cum)
            weight = ending * step[heads, rows]
            from_start = expand(jnp.exp(cum), W, head_dim)
            to_end = expand(weight, W, head_dim)
            x = xbuf[k, rows, :].astype(F32)
            dyf = dy[rows, wide].astype(F32)
            enter, leave = s_ref[b], g_ref[b]
            in_map, out_map = mbuf[rows, :STATE], mbuf[rows, STATE:]
            carried = from_start * dot(out_map, enter, 1, 0)
            pulled = dot(in_map, leave, 1, 0)
            y[rows, wide] = (y[rows, wide].astype(F32) + carried).astype(BF16)
            dxbuf[k, rows, :] = (dxbuf[k, rows, :].astype(F32) + to_end * pulled).astype(BF16)
            xq = head_sums(x * pulled, head_dim)
            gs[heads, rows] = gs1[k, b] + ending * xq
            gc = gc1[k, b] + head_sums(dyf * carried, head_dim) - weight * xq
            place = lax.broadcasted_iota(jnp.int32, gc.shape, 1)
            gc = gc + jnp.where(place == BLOCK - 1, dots[b][:, 0:1], 0.0)
            gd[heads, rows] = triangular(gc, 1)
            acc[rows, :STATE] += dot((x * to_end).astype(BF16), leave, 1, 1)
            acc[rows, STATE:] += dot((dyf * from_start).astype(BF16), enter, 1, 1)
            return carry

        lax.fori_loop(0, NB, block, 0)
        for o in order:
            send_back(k, o).start()
        rbuf[k, head] = dxbuf[k, at(head * TR, TR), :]

    def stage(k, carry):
        @pl.when(k < K)
        def _():
            for o in order:
                recv_x(k, o).wait_recv()
            states(k)

        @pl.when((k >= 1) & (k <= K))
        def _():
            chain(k - 1)

        @pl.when(k >= 2)
        def _():
            carry_over(k - 2)

        @pl.when(k < K)
        def _():
            intra(k)

        return carry

    lax.fori_loop(0, K + 2, stage, 0)

    def send_mapgrad(o):
        return remote(gms.at[at(peer(o) * TR, TR)], gmr.at[head], g_send.at[o], g_recv.at[o], (c, peer(o)))

    def recv_mapgrad(o):
        return remote(gms.at[at(peer(o) * TR, TR)], gmr.at[source(o)], g_send.at[o], g_recv.at[o], (c, peer(o)))

    for b in range(NB):
        rows = slice(b * BLOCK, (b + 1) * BLOCK)
        grad = jnp.where(causal, da[b], 0.0).astype(BF16)
        gms[rows, :STATE] = (acc[rows, :STATE] + dot(grad, mbuf[rows, STATE:], 0, 0)).astype(BF16)
        gms[rows, STATE:] = (acc[rows, STATE:] + dot(grad, mbuf[rows, :STATE], 1, 0)).astype(BF16)
    for o in order:
        send_mapgrad(o).start()
    gmr[head] = gms[at(head * TR, TR), :]

    def send_edge(k, wide):
        return remote(
            hsend.at[k, :, pl.ds(0, wide)], hrecv.at[k, :, pl.ds(0, wide)], h_send.at[k], h_recv.at[k], preceding
        )

    def edge(k, wide):
        @pl.when(index > 0)
        def _():
            send_edge(k, wide).start()

    def arrive_edge(k, wide):
        @pl.when(index < total - 1)
        def _():
            send_edge(k, wide).wait_recv()

        @pl.when(index == total - 1)
        def _():
            hrecv[k] = jnp.zeros(hrecv.shape[1:], F32)

    def unwind(grad_pre, tail, where):
        padded = jnp.concatenate([grad_pre, tail], axis=0)
        out = cw[taps - 1 : taps, where] * grad_pre
        for tap in range(taps - 2, -1, -1):
            begin = taps - 1 - tap
            out = out + cw[tap : tap + 1, where] * padded[begin : begin + TR]
        gin[:, where] = out.astype(BF16)

    def first_rows(k):
        for o in order:
            recv_back(k, o).wait_recv()
        for p in range(H):
            where = at(p * lanes + k * W, W)
            top = rbuf[k, p, :16].astype(F32) * dsil[:16, where].astype(F32)
            hsend[k, :, p * W : (p + 1) * W] = top[:8]
        edge(k, H * W)

    def last_rows(k):
        arrive_edge(k, H * W)
        for p in range(H):
            for i in range(TPC):
                where = at(p * lanes + k * W + i * TILE, TILE)
                inside = slice(i * TILE, (i + 1) * TILE)
                grad_pre = rbuf[k, p, :, inside].astype(F32) * dsil[:, where].astype(F32)
                unwind(grad_pre, hrecv[k, :, p * W + i * TILE : p * W + (i + 1) * TILE], where)

    def final(k, carry):
        @pl.when(k < K)
        def _():
            first_rows(k)

        @pl.when(k >= 1)
        def _():
            last_rows(k - 1)

        return carry

    lax.fori_loop(0, K + 1, final, 0)

    for o in order:
        recv_mapgrad(o).wait_recv()
    parts = []
    for i in range(2 * STATE // TILE):
        inside = slice(i * TILE, (i + 1) * TILE)
        summed = gmr[0, :, inside].astype(F32)
        for p in range(1, H):
            summed = summed + gmr[p, :, inside].astype(F32)
        grad_pre = summed.astype(BF16).astype(F32) * dsil[:, inner + i * TILE : inner + (i + 1) * TILE].astype(F32)
        parts.append(grad_pre)
        hsend[K, :, inside] = grad_pre[:8]
    edge(K, 2 * STATE)
    arrive_edge(K, 2 * STATE)
    for i in range(2 * STATE // TILE):
        inside = slice(i * TILE, (i + 1) * TILE)
        unwind(parts[i], hrecv[K, :, inside], slice(inner + i * TILE, inner + (i + 1) * TILE))

    @pl.when(index < total - 1)
    def _():
        halo_copy.wait_send()

    for o in order:
        send_maps(o).wait_send()
        send_mapgrad(o).wait_send()

    def drain(k, carry):
        for o in order:
            send_x(k, o).wait_send()
            send_back(k, o).wait_send()
        for j in range(TPC):
            @pl.when(owner(k, j) != c)
            def _():
                send_tile(k, j).wait_send()
        mine = (c + total * TPC - k * TPC) % C

        @pl.when(mine < TPC)
        def _():
            def leave(dst, carry):
                @pl.when(dst != c)
                def _():
                    send_enter(k, mine, dst).wait_send()
                return carry

            lax.fori_loop(0, C, leave, 0)

        return carry

    lax.fori_loop(0, K, drain, 0)

    @pl.when(index > 0)
    def _():
        def drain_edges(k, carry):
            send_edge(k, H * W).wait_send()
            return carry

        lax.fori_loop(0, K, drain_edges, 0)
        send_edge(K, 2 * STATE).wait_send()


def local(conv_input, conv_weight, conv_bias, step_size, log_decay, skip_gain, grad_output):
    tok_rows, channels = conv_input.shape
    heads_here, seq_rows = step_size.shape
    lanes = grad_output.shape[1]
    head_dim = lanes // heads_here
    H = lax.axis_size("head")
    C = lax.axis_size("ctx")
    K = heads_here // GROUP
    W = GROUP * head_dim
    NB = seq_rows // BLOCK
    TPC = W // TILE
    packed = 2 * STATE + 2 * GROUP
    skip = jnp.broadcast_to(jnp.repeat(skip_gain, head_dim)[None, :], (GROUP, lanes))
    dma = pltpu.SemaphoreType.DMA
    vmem = pl.BlockSpec(memory_space=pltpu.VMEM)
    return pl.pallas_call(
        partial(mixer_kernel, H, C, head_dim),
        out_shape=[
            jax.ShapeDtypeStruct((seq_rows, lanes), BF16),
            jax.ShapeDtypeStruct((tok_rows, channels), BF16),
            jax.ShapeDtypeStruct((heads_here, seq_rows), F32),
            jax.ShapeDtypeStruct((heads_here, seq_rows), F32),
        ],
        in_specs=[vmem] * 7,
        out_specs=[vmem] * 4,
        scratch_shapes=[
            pltpu.VMEM((16, channels), BF16),
            pltpu.VMEM((K, H, tok_rows, W), BF16),
            pltpu.VMEM((tok_rows, 2 * STATE), BF16),
            pltpu.VMEM((tok_rows, channels), BF16),
            pltpu.VMEM((K, seq_rows, W), BF16),
            pltpu.VMEM((seq_rows, 2 * STATE), BF16),
            pltpu.VMEM((K, NB, GROUP, BLOCK), F32),
            pltpu.VMEM((NB, BLOCK, BLOCK), F32),
            pltpu.VMEM((NB, BLOCK, BLOCK), F32),
            pltpu.VMEM((K, NB, STATE, W), F32),
            pltpu.VMEM((K, NB, STATE, W), F32),
            pltpu.VMEM((K, NB, GROUP, W), F32),
            pltpu.VMEM((STATE, W), F32),
            pltpu.VMEM((STATE, W), F32),
            pltpu.VMEM((GROUP, W), F32),
            pltpu.VMEM((K, TPC, packed, TILE), BF16),
            pltpu.VMEM((K, C, packed, TILE), BF16),
            pltpu.VMEM((K, C, 2 * STATE, TILE), BF16),
            pltpu.VMEM((K, TPC, 2 * STATE, TILE), BF16),
            pltpu.VMEM((NB, STATE, W), BF16),
            pltpu.VMEM((NB, STATE, W), BF16),
            pltpu.VMEM((NB, GROUP, TILE), F32),
            pltpu.VMEM((K, NB, GROUP, BLOCK), F32),
            pltpu.VMEM((K, NB, GROUP, BLOCK), F32),
            pltpu.VMEM((K, seq_rows, W), BF16),
            pltpu.VMEM((K, H, tok_rows, W), BF16),
            pltpu.VMEM((seq_rows, 2 * STATE), F32),
            pltpu.VMEM((seq_rows, 2 * STATE), BF16),
            pltpu.VMEM((H, tok_rows, 2 * STATE), BF16),
            pltpu.VMEM((K + 1, 8, H * W), F32),
            pltpu.VMEM((K + 1, 8, H * W), F32),
            dma((2,)),
            dma((K, H)),
            dma((K, H)),
            dma((H,)),
            dma((H,)),
            dma((K, TPC)),
            dma((K, C)),
            dma((K, C)),
            dma((K, TPC)),
            dma((K, H)),
            dma((K, H)),
            dma((H,)),
            dma((H,)),
            dma((K + 1,)),
            dma((K + 1,)),
        ],
        compiler_params=pltpu.CompilerParams(
            vmem_limit_bytes=VMEM_LIMIT, collective_id=0, has_side_effects=True
        ),
        cost_estimate=pl.CostEstimate(
            flops=30_000_000_000, bytes_accessed=13_000_000, transcendentals=10_000_000
        ),
        name="mixer",
    )(conv_input, conv_weight, conv_bias[None, :], step_size, log_decay, skip, grad_output)


def solution(mesh):
    return jax.shard_map(
        local,
        mesh=mesh,
        in_specs=(
            P(("ctx", "head"), None),
            P(),
            P(),
            P("head", "ctx"),
            P("head", "ctx"),
            P("head"),
            P("ctx", "head"),
        ),
        out_specs=(P("ctx", "head"), P(("ctx", "head"), None), P("head", "ctx"), P("head", "ctx")),
        check_vma=False,
    )
```

time: 220 us -> 136 us (0.62); the launches traced: 216 us -> 136 us
  blocking collectives: 92.1 us -> 0 us
  Pallas kernels: 59.8 us -> 125 us
  waiting for transfers between devices: 20.2 us -> 0 us
  starting transfers between devices: 18.2 us -> 0 us
  other arithmetic: 17.9 us -> 0 us
  local copies, waits for them, and re-layouts: 7.32 us -> 9.95 us
    all_to_all x2 -> x0, blocking collectives: 92.1 us -> none  [the longest x1 46.2 us: local(): got = lax.all_to_all(send, 'head', split_axis=0, concat_axis=0, tiled=True)]
    pallas_call x5 -> x1, Pallas kernels: 59.8 us -> 125 us  [local(): pl.pallas_call(partial(mixer_kernel, H, C, head_dim), out_shape=[jax.Shap...]
    all_to_all x2 -> x0, waiting for transfers between devices: 16.8 us -> none  [columns(): return lax.all_to_all(value, 'ctx', split_axis=0, concat_axis=0, tiled=True)]
    convert_element_type x3 -> x0, other arithmetic: 12.9 us -> none  [the longest x1 5.55 us: local(): activated = activated.astype(BF16)]
    all_to_all x2 -> x0, starting transfers between devices: 11.6 us -> none  [columns(): return lax.all_to_all(value, 'ctx', split_axis=0, concat_axis=0, tiled=True)]
    ppermute x2 -> x0, starting transfers between devices: 6.63 us -> none  [shifted(): return lax.ppermute(value, axis, pairs)]
    ppermute x2 -> x0, waiting for transfers between devices: 3.38 us -> none  [shifted(): return lax.ppermute(value, axis, pairs)]
    unnamed x36 -> x10, local copies, waits for them, and re-layouts: 4.22 us -> 7.11 us
  transfers between devices with their start and end apart: 4 -> 0, of which waited for: 3 -> 0; matrix products, arithmetic and copies ran while one was open for 1% -> 0% of each run, Pallas kernels for 13% -> 0%
where the time goes in v1:
time: 136 us
  Pallas kernels  125 us (92%)
  local copies, waits for them, and re-layouts  9.95 us (7%)
    pallas_call x1, Pallas kernels, local(): pl.pallas_call(partial(mixer_kernel, H, C, head_dim), out_shape=[jax.Shap...  125 us
    unnamed x10, local copies, waits for them, and re-layouts  7.11 us

profile of v1, /device:TPU:9, one launch (start us, length us, event | category | flops | bytes accessed | tf_op | source)
XLA Modules:
  0.0 135.7 jit_solution(6622516708737729736)
XLA Ops:
  0.6 0.7 broadcast_in_dim.14
  1.4 0.1 broadcast_in_dim.15
  1.4 1.4 %broadcast_in_dim.13.cb = f32[1,8448]{1,0:T(1,128)} reshape(f32[8448]{0:T(1024)} %param.9) | data formatting | bytes 67584 | tf_op jit(solution)/shard_map/broadcast_in_dim | solution.py:630
  2.8 0.6 broadcast_in_dim.16.skip
  3.5 125.1 %mixer.1 = (bf16[768,2048]{1,0:T(8,128)(2,1)}, bf16[192,8448]{1,0:T(8,128)(2,1)}, f32[32,768]{1,0:T(8,128)}, f32[32,768]{1,0:T(8,128)}) custom-call(bf16[192,8448]{1,0:T(8,128)(2,1)} %cin.1, f32[4,8448]{1,0:T(4,128)} %cw.1, f32[1,8448]{1,0:T(1,128)} %broadcast_in_dim.13.cb, f32[32,768]{1,0:T(8,128)} %step.1, f32[32,768]{1,0:T(8,128)} %rate.1, ...), custom_call_target="tpu_custom_call" | custom-call | flops 30000001024 | bytes 13000000 | tf_op jit(solution)/shard_map/mixer/pallas_call | solution.py:565
  128.6 0.0 copy-start
  128.6 4.1 %copy.15 = bf16[768,2048]{1,0:T(8,128)(2,1)} copy(bf16[768,2048]{1,0:T(8,128)(2,1)} %get-tuple-element.8) | data formatting | bytes 6291456
  132.7 0.0 copy-done
  132.7 0.0 copy-start.2
  132.7 0.0 copy-start.1
  132.7 1.7 %copy.16 = bf16[192,8448]{1,0:T(8,128)(2,1)} copy(bf16[192,8448]{1,0:T(8,128)(2,1)S(1)} %copy-done) | data formatting | bytes 6488064
  134.4 0.0 copy-done.2
  134.4 0.6 copy.17
  135.1 0.0 copy-done.1
  135.1 0.6 copy.18
Async XLA Ops:
  128.6 4.1 %copy-start = (bf16[192,8448]{1,0:T(8,128)(2,1)S(1)}, bf16[192,8448]{1,0:T(8,128)(2,1)}, u32[]{:S(2)}) copy-start(bf16[192,8448]{1,0:T(8,128)(2,1)} %get-tuple-element.9) | copy-start | bytes 9732100
  132.7 1.7 %copy-start.2 = (f32[32,768]{1,0:T(8,128)S(1)}, f32[32,768]{1,0:T(8,128)}, u32[]{:S(2)}) copy-start(f32[32,768]{1,0:T(8,128)} %get-tuple-element.10) | copy-start | bytes 294916
  132.7 2.3 %copy-start.1 = (f32[32,768]{1,0:T(8,128)S(1)}, f32[32,768]{1,0:T(8,128)}, u32[]{:S(2)}) copy-start(f32[32,768]{1,0:T(8,128)} %get-tuple-element.11) | copy-start | bytes 294916

commit v2 on v1

v2 whole, which is shorter than its diff:
```python
from functools import partial

import jax
import jax.numpy as jnp
from jax import lax
from jax.experimental import pallas as pl
from jax.experimental.pallas import tpu as pltpu
from jax.sharding import PartitionSpec as P

STATE = 128
BLOCK = 256
GROUP = 8
TILE = 128
F32 = jnp.float32
BF16 = jnp.bfloat16
VMEM_LIMIT = 60 * 1024 * 1024
MESH = pl.DeviceIdType.MESH


def dot(a, b, ca, cb):
    return lax.dot_general(
        a, b, (((ca,), (cb,)), ((), ())), preferred_element_type=F32
    )


def head_of_lane(rows, width, head_dim):
    row = lax.broadcasted_iota(jnp.int32, (rows, width), 0)
    lane = lax.broadcasted_iota(jnp.int32, (rows, width), 1)
    return jnp.where(lax.rem(row, GROUP) == lane // head_dim, 1.0, 0.0).astype(BF16)


def expand(rows, width, head_dim):
    high = rows.astype(BF16).astype(F32)
    both = jnp.concatenate([high, rows - high], axis=0).astype(BF16)
    return dot(both, head_of_lane(2 * GROUP, width, head_dim), 0, 0)


def head_sums(value, head_dim):
    pick = head_of_lane(2 * GROUP, value.shape[1], head_dim)
    return dot(pick, value.astype(BF16), 1, 1)[:GROUP]


def triangular(rows, contract):
    length = rows.shape[1]
    row = lax.broadcasted_iota(jnp.int32, (length, length), 0)
    col = lax.broadcasted_iota(jnp.int32, (length, length), 1)
    upper = jnp.where(row <= col, 1.0, 0.0).astype(BF16)
    high = rows.astype(BF16).astype(F32)
    rest = rows - high
    middle = rest.astype(BF16).astype(F32)
    terms = jnp.concatenate([high, middle, rest - middle, jnp.zeros_like(rows)], axis=0)
    sums = dot(terms.astype(BF16), upper, 1, contract)
    return sums[:GROUP] + sums[GROUP : 2 * GROUP] + sums[2 * GROUP : 3 * GROUP]


def at(start, size):
    return pl.ds(pl.multiple_of(start, size), size)


def mixer_kernel(
    H, C, head_dim,
    cin, cw, cb, step, rate, skip, dy,
    y, gin, gs, gd,
    halo, act, actm, dsil, xbuf, mbuf, cums, aff, da, inc, gp, dec,
    t_ref, d_ref, tsend, inbox, outbox, ent, s_ref, g_ref, dots,
    dxbuf, rbuf, acc, gms, gmr, hsend, hrecv,
    halo_send, halo_recv, x_send, x_recv, m_send, m_recv, t_send, t_recv, e_send, e_recv,
    b_send, b_recv, g_send, g_recv, h_send, h_recv,
):
    taps = cw.shape[0]
    TR, channels = cin.shape
    SR, lanes = dy.shape
    K, _, W = xbuf.shape
    NB = SR // BLOCK
    TPC = W // TILE
    inner = H * lanes
    c = lax.axis_index("ctx")
    head = lax.axis_index("head")
    index = c * H + head
    total = C * H
    order = sorted(range(1, H), key=lambda o: abs(o - H // 2))

    def where_is(i):
        return (i // H, i % H)

    following = where_is((index + 1) % total)
    preceding = where_is((index + total - 1) % total)

    barrier = pltpu.get_barrier_semaphore()
    for o in range(1, H):
        pl.semaphore_signal(barrier, inc=1, device_id=(c, (head + o) % H), device_id_type=MESH)
    for o in range(1, C):
        pl.semaphore_signal(barrier, inc=1, device_id=((c + o) % C, head), device_id_type=MESH)
    for who in (following, preceding):
        pl.semaphore_signal(barrier, inc=1, device_id=who, device_id_type=MESH)
    pl.semaphore_wait(barrier, H + C)

    def remote(src, dst, send, recv, who):
        return pltpu.make_async_remote_copy(
            src_ref=src, dst_ref=dst, send_sem=send, recv_sem=recv, device_id=who, device_id_type=MESH
        )

    def send_halo(i, where):
        return remote(
            cin.at[pl.ds(TR - 16, 16), where], halo.at[:, where], halo_send.at[i], halo_recv.at[i], following
        )

    map_lanes = pl.ds(inner, 2 * STATE)

    def chunk_lanes(k, p):
        return at(p * lanes + k * W, W)

    @pl.when(index < total - 1)
    def _():
        send_halo(K * H, map_lanes).start()

        def start_halo(i, carry):
            send_halo(i, chunk_lanes(i // H, i % H)).start()
            return carry

        lax.fori_loop(0, K * H, start_halo, 0)

    @pl.when(index == 0)
    def _():
        halo[...] = jnp.zeros_like(halo)

    @pl.when(index > 0)
    def _():
        send_halo(K * H, map_lanes).wait_recv()

    def convolve(col):
        where = at(col, TILE)
        body = cin[:, where].astype(F32)
        padded = jnp.concatenate([halo[:, where].astype(F32)[8:], body], axis=0)
        first = 8 - (taps - 1)
        pre = cb[pl.ds(col // TILE, 1), :] + cw[0:1, where] * padded[first : first + TR]
        for tap in range(1, taps):
            pre = pre + cw[tap : tap + 1, where] * padded[first + tap : first + tap + TR]
        sig = 0.5 * jnp.tanh(0.5 * pre) + 0.5
        value = pre * sig
        dsil[:, where] = (sig + value * (1.0 - sig)).astype(BF16)
        return value.astype(BF16)

    def peer(o):
        return (head + o) % H

    def source(o):
        return (head + H - o) % H

    def send_maps(o):
        return remote(actm, mbuf.at[at(head * TR, TR)], m_send.at[o], m_recv.at[o], (c, peer(o)))

    def recv_maps(o):
        return remote(actm, mbuf.at[at(source(o) * TR, TR)], m_send.at[o], m_recv.at[o], (c, peer(o)))

    def send_x(k, o):
        return remote(
            act.at[k, peer(o)], xbuf.at[k, at(head * TR, TR)], x_send.at[k, o], x_recv.at[k, o], (c, peer(o))
        )

    def recv_x(k, o):
        return remote(
            act.at[k, peer(o)], xbuf.at[k, at(source(o) * TR, TR)], x_send.at[k, o], x_recv.at[k, o], (c, peer(o))
        )

    for i in range(2 * STATE // TILE):
        actm[:, i * TILE : (i + 1) * TILE] = convolve(inner + i * TILE)
    for o in order:
        send_maps(o).start()
    mbuf[at(head * TR, TR), :] = actm[...]

    def conv_chunk(k, carry):
        @pl.when(index > 0)
        def _():
            for p in range(H):
                send_halo(k * H + p, chunk_lanes(k, p)).wait_recv()

        for o in order + [0]:
            p = peer(o)
            for i in range(TPC):
                value = convolve(p * lanes + k * W + i * TILE)
                if o:
                    act[k, p, :, i * TILE : (i + 1) * TILE] = value
                else:
                    xbuf[k, at(head * TR, TR), i * TILE : (i + 1) * TILE] = value
            if o:
                send_x(k, o).start()
        return carry

    lax.fori_loop(0, K, conv_chunk, 0)

    def sums_chunk(k, carry):
        for b in range(NB):
            cums[k, b] = triangular(rate[at(k * GROUP, GROUP), b * BLOCK : (b + 1) * BLOCK], 0)
        return carry

    lax.fori_loop(0, K, sums_chunk, 0)

    for o in order:
        recv_maps(o).wait_recv()

    row = lax.broadcasted_iota(jnp.int32, (BLOCK, BLOCK), 0)
    col = lax.broadcasted_iota(jnp.int32, (BLOCK, BLOCK), 1)
    causal = row >= col
    for b in range(NB):
        m = mbuf[b * BLOCK : (b + 1) * BLOCK]
        aff[b] = jnp.where(causal, dot(m[:, STATE:], m[:, :STATE], 1, 1), 0.0)
        da[b] = jnp.zeros((BLOCK, BLOCK), F32)
    acc[...] = jnp.zeros_like(acc)

    stride = C // TPC

    def owner(k, j):
        return j * stride + (j + k) % stride

    def send_tile(q, k, j):
        return remote(
            tsend.at[q, k, j], inbox.at[q, k, c], t_send.at[q, k, j], t_recv.at[q, k, c], (owner(k, j), head)
        )

    def recv_tile(q, k, src):
        return remote(tsend.at[q, k, 0], inbox.at[q, k, src], t_send.at[q, k, 0], t_recv.at[q, k, src], (src, head))

    def pass_on(q, k, decay):
        high = decay.astype(BF16).astype(F32)
        both = jnp.concatenate([high, decay - high], axis=0).astype(BF16)
        for j in range(TPC):
            where = slice(j * TILE, (j + 1) * TILE)
            tsend[q, k, j, :STATE] = t_ref[:, where].astype(BF16)
            tsend[q, k, j, STATE:] = both[:, where]
        for j in range(TPC):
            @pl.when(owner(k, j) == c)
            def _():
                inbox[q, k, c] = tsend[q, k, j]

            @pl.when(owner(k, j) != c)
            def _():
                send_tile(q, k, j).start()

    def pulls(k, carry):
        t_ref[...] = jnp.zeros_like(t_ref)
        d_ref[k] = jnp.ones(d_ref.shape[1:], F32)

        def block(b, carry):
            rows = at(b * BLOCK, BLOCK)
            from_start = expand(jnp.exp(cums[k, b]), W, head_dim)
            dyw = (dy[rows, at(k * W, W)].astype(F32) * from_start).astype(BF16)
            grad = dot(mbuf[rows, STATE:], dyw, 0, 0)
            last_dec = from_start[BLOCK - 1 :]
            gp[k, b] = grad
            dec[k, b] = jnp.broadcast_to(last_dec, (GROUP, W))
            t_ref[...] = t_ref[...] + d_ref[k, 0:1] * grad
            d_ref[k] = d_ref[k] * last_dec
            return carry

        lax.fori_loop(0, NB, block, 0)
        pass_on(1, k, d_ref[k])
        return carry

    lax.fori_loop(0, K, pulls, 0)

    def states(k):
        t_ref[...] = jnp.zeros_like(t_ref)

        def block(b, carry):
            rows = at(b * BLOCK, BLOCK)
            cum = cums[k, b]
            to_end = expand(jnp.exp(cum[:, BLOCK - 1 :] - cum) * step[at(k * GROUP, GROUP), rows], W, head_dim)
            xw = (xbuf[k, rows, :].astype(F32) * to_end).astype(BF16)
            more = dot(mbuf[rows, :STATE], xw, 0, 0)
            inc[k, b] = more
            t_ref[...] = t_ref[...] * dec[k, b, 0:1] + more
            return carry

        lax.fori_loop(0, NB, block, 0)
        pass_on(0, k, d_ref[k])

    def send_enter(q, k, j, dst):
        return remote(outbox.at[q, k, dst], ent.at[q, k, j], e_send.at[q, k, dst], e_recv.at[q, k, j], (dst, head))

    def chain(q, k):
        j = c // stride

        @pl.when(c == owner(k, j))
        def _():
            def arrive(src, carry):
                @pl.when(src != c)
                def _():
                    recv_tile(q, k, src).wait_recv()
                return carry

            lax.fori_loop(0, C, arrive, 0)

            def follow(i, state):
                i = C - 1 - i if q else i
                outbox[q, k, i] = state.astype(BF16)
                both = inbox[q, k, i, STATE:].astype(F32)
                return (both[0:1] + both[GROUP : GROUP + 1]) * state + inbox[q, k, i, :STATE].astype(F32)

            lax.fori_loop(0, C, follow, jnp.zeros((STATE, TILE), F32))

            def leave(dst, carry):
                @pl.when(dst != c)
                def _():
                    send_enter(q, k, j, dst).start()
                return carry

            lax.fori_loop(0, C, leave, 0)
            ent[q, k, j] = outbox[q, k, c]

    half = BLOCK // 2
    pair = 2 * head_dim

    def intra(k):
        first = lax.broadcasted_iota(jnp.int32, (half, pair), 1) < head_dim

        def each(value):
            none = jnp.zeros_like(value)
            return jnp.concatenate([jnp.where(first, value, none), jnp.where(first, none, value)], axis=0)

        def block(b, carry):
            rows = at(b * BLOCK, BLOCK)
            cum = cums[k, b]
            cum_col = cum.T
            dyb = dy[rows, at(k * W, W)]
            steps = expand(step[at(k * GROUP, GROUP), rows], W, head_dim)
            xsf = xbuf[k, rows, :].astype(F32) * steps
            xs = xsf.astype(BF16)
            middle = cum[:, half - 1 : half]
            until = expand(jnp.exp(middle - cum[:, :half]), W, head_dim)
            since = expand(jnp.exp(cum[:, half:] - middle), W, head_dim)
            early = (xsf[:half] * until).astype(BF16)
            late = (dyb[half:].astype(F32) * since).astype(BF16)
            across = aff[b, half:, :half].astype(BF16)
            ins_late = since * dot(across, early, 1, 0)
            back_early = until * dot(across, late, 0, 0)
            da[b, half:, :half] += dot(late, early, 1, 1)
            for part in range(2):
                side = slice(part * half, (part + 1) * half)
                near = aff[b, side, side]
                near_da = jnp.zeros((half, half), F32)
                for p in range(GROUP // 2):
                    where = slice(p * pair, (p + 1) * pair)
                    xs_p, dy_p = each(xs[side, where]), dyb[side, where]
                    decays = [
                        jnp.exp(jnp.minimum(cum_col[side, h : h + 1] - cum[h : h + 1, side], 0.0))
                        for h in (2 * p, 2 * p + 1)
                    ]
                    weights = [(near * decay).astype(BF16) for decay in decays]
                    ins = dot(jnp.concatenate(weights, axis=1), xs_p, 1, 0)
                    back = dot(jnp.concatenate(weights, axis=0), each(dy_p), 0, 0)
                    both = dot(dy_p, xs_p, 1, 1)
                    near_da = near_da + both[:, :half] * decays[0] + both[:, half:] * decays[1]
                    if part:
                        ins = ins + ins_late[:, where]
                    else:
                        back = back + back_early[:, where]
                    y[at(b * BLOCK + part * half, half), at(k * W + p * pair, pair)] = ins.astype(BF16)
                    dxbuf[k, at(b * BLOCK + part * half, half), where] = back.astype(BF16)
                da[b, side, side] += near_da
            return carry

        lax.fori_loop(0, NB, block, 0)

    def send_back(k, o):
        return remote(
            dxbuf.at[k, at(peer(o) * TR, TR)], rbuf.at[k, head], b_send.at[k, o], b_recv.at[k, o], (c, peer(o))
        )

    def recv_back(k, o):
        return remote(
            dxbuf.at[k, at(peer(o) * TR, TR)], rbuf.at[k, source(o)], b_send.at[k, o], b_recv.at[k, o], (c, peer(o))
        )

    def carry_over(k):
        for j in range(TPC):
            @pl.when(owner(k, j) != c)
            def _():
                for q in range(2):
                    remote(
                        outbox.at[q, k, 0], ent.at[q, k, j], e_send.at[q, k, 0], e_recv.at[q, k, j], (owner(k, j), head)
                    ).wait_recv()

        state = jnp.concatenate([ent[0, k, j] for j in range(TPC)], axis=1).astype(F32)
        grad = jnp.concatenate([ent[1, k, j] for j in range(TPC)], axis=1).astype(F32)
        grads = [None] * NB
        for b in range(NB - 1, -1, -1):
            grads[b] = grad
            g_ref[b] = grad.astype(BF16)
            if b > 0:
                grad = dec[k, b, 0:1] * grad + gp[k, b]
        for b in range(NB):
            s_ref[b] = state.astype(BF16)
            state = dec[k, b, 0:1] * state + inc[k, b]
            both = jnp.sum(state * grads[b], axis=0, keepdims=True)
            dots[b] = head_sums(jnp.broadcast_to(both, (TILE, W)), head_dim)

        lane_head = lax.broadcasted_iota(jnp.int32, (1, W), 1) // head_dim
        gain = jnp.zeros((1, W), F32)
        for h in range(GROUP):
            gain = jnp.where(lane_head == h, skip[k * GROUP + h], gain)

        def block(turn, carry):
            b = jnp.where(head < H // 2, NB - 1 - turn, turn)
            rows = at(b * BLOCK, BLOCK)
            heads = at(k * GROUP, GROUP)
            wide = at(k * W, W)
            cum = cums[k, b]
            sizes = step[heads, rows]
            from_start = expand(jnp.exp(cum), W, head_dim)
            ending = expand(jnp.exp(cum[:, BLOCK - 1 :] - cum), W, head_dim)
            steps = expand(sizes, W, head_dim)
            x = xbuf[k, rows, :].astype(F32)
            dyf = dy[rows, wide].astype(F32)
            enter, leave = s_ref[b], g_ref[b]
            in_map, out_map = mbuf[rows, :STATE], mbuf[rows, STATE:]
            out = y[rows, wide].astype(F32) + from_start * dot(out_map, enter, 1, 0)
            back = dxbuf[k, rows, :].astype(F32) + ending * dot(in_map, leave, 1, 0)
            y[rows, wide] = (out + gain * x).astype(BF16)
            dxbuf[k, rows, :] = (steps * back + gain * dyf).astype(BF16)
            by_step = head_sums(x * back, head_dim)
            gs[heads, rows] = by_step
            gc = head_sums(dyf * out, head_dim) - sizes * by_step
            place = lax.broadcasted_iota(jnp.int32, gc.shape, 1)
            gc = gc + jnp.where(place == BLOCK - 1, dots[b][:, 0:1], 0.0)
            gd[heads, rows] = triangular(gc, 1)
            acc[rows, :STATE] += dot((x * steps * ending).astype(BF16), leave, 1, 1)
            acc[rows, STATE:] += dot((dyf * from_start).astype(BF16), enter, 1, 1)
            for o in order:
                low, high = peer(o) * TR // BLOCK, (peer(o) * TR + TR - 1) // BLOCK

                @pl.when(b == jnp.where(head < H // 2, low, high))
                def _():
                    send_back(k, o).start()
            return carry

        lax.fori_loop(0, NB, block, 0)
        rbuf[k, head] = dxbuf[k, at(head * TR, TR), :]

    def send_mapgrad(o):
        return remote(gms.at[at(peer(o) * TR, TR)], gmr.at[head], g_send.at[o], g_recv.at[o], (c, peer(o)))

    def recv_mapgrad(o):
        return remote(gms.at[at(peer(o) * TR, TR)], gmr.at[source(o)], g_send.at[o], g_recv.at[o], (c, peer(o)))

    def send_edge(k, wide):
        return remote(
            hsend.at[k, :, pl.ds(0, wide)], hrecv.at[k, :, pl.ds(0, wide)], h_send.at[k], h_recv.at[k], preceding
        )

    def edge(k, wide):
        @pl.when(index > 0)
        def _():
            send_edge(k, wide).start()

    def arrive_edge(k, wide):
        @pl.when(index < total - 1)
        def _():
            send_edge(k, wide).wait_recv()

        @pl.when(index == total - 1)
        def _():
            hrecv[k] = jnp.zeros(hrecv.shape[1:], F32)

    def unwind(grad_pre, tail, where):
        padded = jnp.concatenate([grad_pre, tail], axis=0)
        out = cw[taps - 1 : taps, where] * grad_pre
        for tap in range(taps - 2, -1, -1):
            begin = taps - 1 - tap
            out = out + cw[tap : tap + 1, where] * padded[begin : begin + TR]
        gin[:, where] = out.astype(BF16)

    def first_rows(k):
        for o in order:
            recv_back(k, o).wait_recv()
        for p in range(H):
            where = at(p * lanes + k * W, W)
            top = rbuf[k, p, :16].astype(F32) * dsil[:16, where].astype(F32)
            hsend[k, :, p * W : (p + 1) * W] = top[:8]
        edge(k, H * W)

    def last_rows(k):
        arrive_edge(k, H * W)
        for p in range(H):
            for i in range(TPC):
                where = at(p * lanes + k * W + i * TILE, TILE)
                inside = slice(i * TILE, (i + 1) * TILE)
                grad_pre = rbuf[k, p, :, inside].astype(F32) * dsil[:, where].astype(F32)
                unwind(grad_pre, hrecv[k, :, p * W + i * TILE : p * W + (i + 1) * TILE], where)

    def stage(k, carry):
        @pl.when(k < K)
        def _():
            for o in order:
                recv_x(k, o).wait_recv()
            states(k)
            chain(1, k)
            intra(k)
            chain(0, k)

        @pl.when(k >= 1)
        def _():
            carry_over(k - 1)

        @pl.when(k >= 2)
        def _():
            first_rows(k - 2)

        @pl.when(k >= 3)
        def _():
            last_rows(k - 3)

        return carry

    lax.fori_loop(0, K + 1, stage, 0)

    for b in range(NB):
        rows = slice(b * BLOCK, (b + 1) * BLOCK)
        grad = jnp.where(causal, da[b], 0.0).astype(BF16)
        gms[rows, :STATE] = (acc[rows, :STATE] + dot(grad, mbuf[rows, STATE:], 0, 0)).astype(BF16)
        gms[rows, STATE:] = (acc[rows, STATE:] + dot(grad, mbuf[rows, :STATE], 1, 0)).astype(BF16)
    for o in order:
        send_mapgrad(o).start()
    gmr[head] = gms[at(head * TR, TR), :]

    for k in range(max(K - 2, 0), K - 1):
        last_rows(k)
    first_rows(K - 1)
    for o in order:
        recv_mapgrad(o).wait_recv()
    parts = []
    for i in range(2 * STATE // TILE):
        inside = slice(i * TILE, (i + 1) * TILE)
        summed = gmr[0, :, inside].astype(F32)
        for p in range(1, H):
            summed = summed + gmr[p, :, inside].astype(F32)
        grad_pre = summed.astype(BF16).astype(F32) * dsil[:, inner + i * TILE : inner + (i + 1) * TILE].astype(F32)
        parts.append(grad_pre)
        hsend[K, :, inside] = grad_pre[:8]
    edge(K, 2 * STATE)
    last_rows(K - 1)
    arrive_edge(K, 2 * STATE)
    for i in range(2 * STATE // TILE):
        inside = slice(i * TILE, (i + 1) * TILE)
        unwind(parts[i], hrecv[K, :, inside], slice(inner + i * TILE, inner + (i + 1) * TILE))

    @pl.when(index < total - 1)
    def _():
        send_halo(K * H, map_lanes).wait_send()

        def drain_halo(i, carry):
            send_halo(i, chunk_lanes(i // H, i % H)).wait_send()
            return carry

        lax.fori_loop(0, K * H, drain_halo, 0)

    for o in order:
        send_maps(o).wait_send()
        send_mapgrad(o).wait_send()

    def drain(k, carry):
        for o in order:
            send_x(k, o).wait_send()
            send_back(k, o).wait_send()
        for q in range(2):
            for j in range(TPC):
                @pl.when(owner(k, j) != c)
                def _():
                    send_tile(q, k, j).wait_send()

        @pl.when(c == owner(k, c // stride))
        def _():
            def leave(dst, carry):
                @pl.when(dst != c)
                def _():
                    for q in range(2):
                        send_enter(q, k, c // stride, dst).wait_send()
                return carry

            lax.fori_loop(0, C, leave, 0)

        return carry

    lax.fori_loop(0, K, drain, 0)

    @pl.when(index > 0)
    def _():
        def drain_edges(k, carry):
            send_edge(k, H * W).wait_send()
            return carry

        lax.fori_loop(0, K, drain_edges, 0)
        send_edge(K, 2 * STATE).wait_send()


def local(conv_input, conv_weight, conv_bias, step_size, log_decay, skip_gain, grad_output):
    tok_rows, channels = conv_input.shape
    heads_here, seq_rows = step_size.shape
    lanes = grad_output.shape[1]
    head_dim = lanes // heads_here
    H = lax.axis_size("head")
    C = lax.axis_size("ctx")
    K = heads_here // GROUP
    W = GROUP * head_dim
    NB = seq_rows // BLOCK
    TPC = W // TILE
    packed = STATE + 2 * GROUP
    dma = pltpu.SemaphoreType.DMA
    vmem = pl.BlockSpec(memory_space=pltpu.VMEM)
    return pl.pallas_call(
        partial(mixer_kernel, H, C, head_dim),
        out_shape=[
            jax.ShapeDtypeStruct((seq_rows, lanes), BF16),
            jax.ShapeDtypeStruct((tok_rows, channels), BF16),
            jax.ShapeDtypeStruct((heads_here, seq_rows), F32),
            jax.ShapeDtypeStruct((heads_here, seq_rows), F32),
        ],
        in_specs=[vmem] * 5 + [pl.BlockSpec(memory_space=pltpu.SMEM), vmem],
        out_specs=[vmem] * 4,
        scratch_shapes=[
            pltpu.VMEM((16, channels), BF16),
            pltpu.VMEM((K, H, tok_rows, W), BF16),
            pltpu.VMEM((tok_rows, 2 * STATE), BF16),
            pltpu.VMEM((tok_rows, channels), BF16),
            pltpu.VMEM((K, seq_rows, W), BF16),
            pltpu.VMEM((seq_rows, 2 * STATE), BF16),
            pltpu.VMEM((K, NB, GROUP, BLOCK), F32),
            pltpu.VMEM((NB, BLOCK, BLOCK), F32),
            pltpu.VMEM((NB, BLOCK, BLOCK), F32),
            pltpu.VMEM((K, NB, STATE, W), F32),
            pltpu.VMEM((K, NB, STATE, W), F32),
            pltpu.VMEM((K, NB, GROUP, W), F32),
            pltpu.VMEM((STATE, W), F32),
            pltpu.VMEM((K, GROUP, W), F32),
            pltpu.VMEM((2, K, TPC, packed, TILE), BF16),
            pltpu.VMEM((2, K, C, packed, TILE), BF16),
            pltpu.VMEM((2, K, C, STATE, TILE), BF16),
            pltpu.VMEM((2, K, TPC, STATE, TILE), BF16),
            pltpu.VMEM((NB, STATE, W), BF16),
            pltpu.VMEM((NB, STATE, W), BF16),
            pltpu.VMEM((NB, GROUP, TILE), F32),
            pltpu.VMEM((K, seq_rows, W), BF16),
            pltpu.VMEM((K, H, tok_rows, W), BF16),
            pltpu.VMEM((seq_rows, 2 * STATE), F32),
            pltpu.VMEM((seq_rows, 2 * STATE), BF16),
            pltpu.VMEM((H, tok_rows, 2 * STATE), BF16),
            pltpu.VMEM((K + 1, 8, H * W), F32),
            pltpu.VMEM((K + 1, 8, H * W), F32),
            dma((K * H + 1,)),
            dma((K * H + 1,)),
            dma((K, H)),
            dma((K, H)),
            dma((H,)),
            dma((H,)),
            dma((2, K, TPC)),
            dma((2, K, C)),
            dma((2, K, C)),
            dma((2, K, TPC)),
            dma((K, H)),
            dma((K, H)),
            dma((H,)),
            dma((H,)),
            dma((K + 1,)),
            dma((K + 1,)),
        ],
        compiler_params=pltpu.CompilerParams(
            vmem_limit_bytes=VMEM_LIMIT, collective_id=0, has_side_effects=True
        ),
        cost_estimate=pl.CostEstimate(
            flops=30_000_000_000, bytes_accessed=13_000_000, transcendentals=10_000_000
        ),
        name="mixer",
    )(conv_input, conv_weight, conv_bias.reshape(-1, TILE), step_size, log_decay, skip_gain, grad_output)


def solution(mesh):
    return jax.shard_map(
        local,
        mesh=mesh,
        in_specs=(
            P(("ctx", "head"), None),
            P(),
            P(),
            P("head", "ctx"),
            P("head", "ctx"),
            P("head"),
            P("ctx", "head"),
        ),
        out_specs=(P("ctx", "head"), P(("ctx", "head"), None), P("head", "ctx"), P("head", "ctx")),
        check_vma=False,
    )
```

time: 136 us -> 113 us (0.83)
  Pallas kernels: 125 us -> 105 us
  local copies, waits for them, and re-layouts: 9.95 us -> 7.11 us
    pallas_call x1, Pallas kernels: 125 us -> 105 us  [local(): pl.pallas_call(partial(mixer_kernel, H, C, head_dim), out_shape=[jax.Shap...]
    broadcast_in_dim x4 -> x0, local copies, waits for them, and re-layouts: 2.84 us -> none  [the longest x1 1.41 us: local(): conv_bias[None, :]]
where the time goes in v2:
time: 113 us
  Pallas kernels  105 us (93%)
  local copies, waits for them, and re-layouts  7.11 us (6%)
    pallas_call x1, Pallas kernels, local(): pl.pallas_call(partial(mixer_kernel, H, C, head_dim), out_shape=[jax.Shap...  105 us
    unnamed x10, local copies, waits for them, and re-layouts  7.11 us

profile of v2, /device:TPU:9, one launch (start us, length us, event | category | flops | bytes accessed | tf_op | source)
XLA Modules:
  0.0 112.5 jit_solution(18105847285999266226)
XLA Ops:
  0.6 104.8 %mixer.1 = (bf16[768,2048]{1,0:T(8,128)(2,1)}, bf16[192,8448]{1,0:T(8,128)(2,1)}, f32[32,768]{1,0:T(8,128)}, f32[32,768]{1,0:T(8,128)}) custom-call(bf16[192,8448]{1,0:T(8,128)(2,1)} %cin.1, f32[4,8448]{1,0:T(4,128)} %cw.1, f32[66,128]{1,0:T(8,128)} %bitcast.1, f32[32,768]{1,0:T(8,128)} %step.1, f32[32,768]{1,0:T(8,128)} %rate.1, f32[32]{0:T(128)} %skip.1, ...), custom_call_target="tpu_custom_call" | custom-call | flops 30000001024 | bytes 13000000 | tf_op jit(solution)/shard_map/mixer/pallas_call | solution.py:610
  105.4 0.0 copy-start
  105.4 4.1 %copy.15 = bf16[768,2048]{1,0:T(8,128)(2,1)} copy(bf16[768,2048]{1,0:T(8,128)(2,1)} %get-tuple-element.8) | data formatting | bytes 6291456
  109.5 0.0 copy-done
  109.5 0.0 copy-start.2
  109.5 0.0 copy-start.1
  109.6 1.7 %copy.16 = bf16[192,8448]{1,0:T(8,128)(2,1)} copy(bf16[192,8448]{1,0:T(8,128)(2,1)S(1)} %copy-done) | data formatting | bytes 6488064
  111.2 0.0 copy-done.2
  111.2 0.6 copy.17
  111.9 0.0 copy-done.1
  111.9 0.6 copy.18
Async XLA Ops:
  105.4 4.1 %copy-start = (bf16[192,8448]{1,0:T(8,128)(2,1)S(1)}, bf16[192,8448]{1,0:T(8,128)(2,1)}, u32[]{:S(2)}) copy-start(bf16[192,8448]{1,0:T(8,128)(2,1)} %get-tuple-element.9) | copy-start | bytes 9732100
  109.5 1.7 %copy-start.2 = (f32[32,768]{1,0:T(8,128)S(1)}, f32[32,768]{1,0:T(8,128)}, u32[]{:S(2)}) copy-start(f32[32,768]{1,0:T(8,128)} %get-tuple-element.10) | copy-start | bytes 294916
  109.5 2.3 %copy-start.1 = (f32[32,768]{1,0:T(8,128)S(1)}, f32[32,768]{1,0:T(8,128)}, u32[]{:S(2)}) copy-start(f32[32,768]{1,0:T(8,128)} %get-tuple-element.11) | copy-start | bytes 294916

commit v3 on v2

--- a/solution.py
+++ b/solution.py
@@ -59,12 +59,12 @@
 
 def mixer_kernel(
     H, C, head_dim,
-    cin, cw, cb, step, rate, skip, dy,
-    y, gin, gs, gd,
-    halo, act, actm, dsil, xbuf, mbuf, cums, aff, da, inc, gp, dec,
+    cin, cw, cb, step, rate, skip, dy_hbm,
+    y_hbm, gin_hbm, gs, gd,
+    dy, y, gin, halo, act, actm, dsil, xbuf, mbuf, cums, aff, da, inc, gp, dec,
     t_ref, d_ref, tsend, inbox, outbox, ent, s_ref, g_ref, dots,
     dxbuf, rbuf, acc, gms, gmr, hsend, hrecv,
-    halo_send, halo_recv, x_send, x_recv, m_send, m_recv, t_send, t_recv, e_send, e_recv,
+    dy_sem, y_sem, gin_sem, halo_send, halo_recv, x_send, x_recv, m_send, m_recv, t_send, t_recv, e_send, e_recv,
     b_send, b_recv, g_send, g_recv, h_send, h_recv,
 ):
     taps = cw.shape[0]
@@ -86,6 +86,8 @@
     following = where_is((index + 1) % total)
     preceding = where_is((index + total - 1) % total)
 
+    dy_copy = pltpu.make_async_copy(dy_hbm, dy, dy_sem)
+    dy_copy.start()
     barrier = pltpu.get_barrier_semaphore()
     for o in range(1, H):
         pl.semaphore_signal(barrier, inc=1, device_id=(c, (head + o) % H), device_id_type=MESH)
@@ -257,6 +259,7 @@
         pass_on(1, k, d_ref[k])
         return carry
 
+    dy_copy.wait()
     lax.fori_loop(0, K, pulls, 0)
 
     def states(k):
@@ -372,6 +375,13 @@
             dxbuf.at[k, at(peer(o) * TR, TR)], rbuf.at[k, source(o)], b_send.at[k, o], b_recv.at[k, o], (c, peer(o))
         )
 
+    def store_y(k):
+        wide = at(k * W, W)
+        return pltpu.make_async_copy(y.at[:, wide], y_hbm.at[:, wide], y_sem.at[k])
+
+    def store_gin(i, where):
+        return pltpu.make_async_copy(gin.at[:, where], gin_hbm.at[:, where], gin_sem.at[i])
+
     def carry_over(k):
         for j in range(TPC):
             @pl.when(owner(k, j) != c)
@@ -435,6 +445,7 @@
             return carry
 
         lax.fori_loop(0, NB, block, 0)
+        store_y(k).start()
         rbuf[k, head] = dxbuf[k, at(head * TR, TR), :]
 
     def send_mapgrad(o):
@@ -487,6 +498,7 @@
                 inside = slice(i * TILE, (i + 1) * TILE)
                 grad_pre = rbuf[k, p, :, inside].astype(F32) * dsil[:, where].astype(F32)
                 unwind(grad_pre, hrecv[k, :, p * W + i * TILE : p * W + (i + 1) * TILE], where)
+            store_gin(k * H + p, chunk_lanes(k, p)).start()
 
     def stage(k, carry):
         @pl.when(k < K)
@@ -544,6 +556,8 @@
         inside = slice(i * TILE, (i + 1) * TILE)
         unwind(parts[i], hrecv[K, :, inside], slice(inner + i * TILE, inner + (i + 1) * TILE))
 
+    store_gin(K * H, map_lanes).start()
+
     @pl.when(index < total - 1)
     def _():
         send_halo(K * H, map_lanes).wait_send()
@@ -583,6 +597,15 @@
 
     lax.fori_loop(0, K, drain, 0)
 
+    def stored(k, carry):
+        store_y(k).wait()
+        for p in range(H):
+            store_gin(k * H + p, chunk_lanes(k, p)).wait()
+        return carry
+
+    lax.fori_loop(0, K, stored, 0)
+    store_gin(K * H, map_lanes).wait()
+
     @pl.when(index > 0)
     def _():
         def drain_edges(k, carry):
@@ -591,6 +614,41 @@
 
         lax.fori_loop(0, K, drain_edges, 0)
         send_edge(K, 2 * STATE).wait_send()
+
+
+def hand_on_kernel(count, *refs):
+    ins, outs, held = refs[:count], refs[count : 2 * count], refs[2 * count : 3 * count]
+    in_sem, out_sem = refs[3 * count :]
+    loads, stores = [], []
+    for source, target, keep in zip(ins, outs, held):
+        rows = source.shape[0]
+        pieces = 6 if rows % 96 == 0 else 1
+        for i in range(pieces):
+            part = pl.ds(i * (rows // pieces), rows // pieces)
+            loads.append(pltpu.make_async_copy(source.at[part], keep.at[part], in_sem.at[len(loads)]))
+            stores.append(pltpu.make_async_copy(keep.at[part], target.at[part], out_sem.at[len(stores)]))
+    for load in loads:
+        load.start()
+    for load, store in zip(loads, stores):
+        load.wait()
+        store.start()
+    for store in stores:
+        store.wait()
+
+
+def hand_on(arrays):
+    anywhere = pl.BlockSpec(memory_space=pl.ANY)
+    count = len(arrays)
+    return pl.pallas_call(
+        partial(hand_on_kernel, count),
+        out_shape=[jax.ShapeDtypeStruct(a.shape, a.dtype) for a in arrays],
+        in_specs=[anywhere] * count,
+        out_specs=[anywhere] * count,
+        scratch_shapes=[pltpu.VMEM(a.shape, a.dtype) for a in arrays]
+        + [pltpu.SemaphoreType.DMA((6 * count,))] * 2,
+        compiler_params=pltpu.CompilerParams(vmem_limit_bytes=VMEM_LIMIT),
+        name="hand_on",
+    )(*arrays)
 
 
 def local(conv_input, conv_weight, conv_bias, step_size, log_decay, skip_gain, grad_output):
@@ -607,7 +665,7 @@
     packed = STATE + 2 * GROUP
     dma = pltpu.SemaphoreType.DMA
     vmem = pl.BlockSpec(memory_space=pltpu.VMEM)
-    return pl.pallas_call(
+    results = pl.pallas_call(
         partial(mixer_kernel, H, C, head_dim),
         out_shape=[
             jax.ShapeDtypeStruct((seq_rows, lanes), BF16),
@@ -615,9 +673,12 @@
             jax.ShapeDtypeStruct((heads_here, seq_rows), F32),
             jax.ShapeDtypeStruct((heads_here, seq_rows), F32),
         ],
-        in_specs=[vmem] * 5 + [pl.BlockSpec(memory_space=pltpu.SMEM), vmem],
-        out_specs=[vmem] * 4,
+        in_specs=[vmem] * 5 + [pl.BlockSpec(memory_space=pltpu.SMEM), pl.BlockSpec(memory_space=pl.ANY)],
+        out_specs=[pl.BlockSpec(memory_space=pl.ANY)] * 2 + [vmem] * 2,
         scratch_shapes=[
+            pltpu.VMEM((seq_rows, lanes), BF16),
+            pltpu.VMEM((seq_rows, lanes), BF16),
+            pltpu.VMEM((tok_rows, channels), BF16),
             pltpu.VMEM((16, channels), BF16),
             pltpu.VMEM((K, H, tok_rows, W), BF16),
             pltpu.VMEM((tok_rows, 2 * STATE), BF16),
@@ -646,6 +707,9 @@
             pltpu.VMEM((H, tok_rows, 2 * STATE), BF16),
             pltpu.VMEM((K + 1, 8, H * W), F32),
             pltpu.VMEM((K + 1, 8, H * W), F32),
+            dma,
+            dma((K,)),
+            dma((K * H + 1,)),
             dma((K * H + 1,)),
             dma((K * H + 1,)),
             dma((K, H)),
@@ -671,6 +735,7 @@
         ),
         name="mixer",
     )(conv_input, conv_weight, conv_bias.reshape(-1, TILE), step_size, log_decay, skip_gain, grad_output)
+    return tuple(hand_on(results))
 
 
 def solution(mesh):

time: 113 us -> 108 us (0.956)
  local copies, waits for them, and re-layouts: 7.11 us -> 0 us
  Pallas kernels: 105 us -> 108 us
    unnamed x10 -> x0, local copies, waits for them, and re-layouts: 7.11 us -> none
    pallas_call x0 -> x1, Pallas kernels: none -> 5.77 us  [hand_on(): pl.pallas_call(partial(hand_on_kernel, count), out_shape=[jax.ShapeDtypeS...]
    pallas_call x1, Pallas kernels: 105 us -> 102 us  [local(): pl.pallas_call(partial(mixer_kernel, H, C, head_dim), out_shape=[jax.Shap...]
where the time goes in v3:
time: 108 us
  Pallas kernels  108 us (100%)
    pallas_call x1, Pallas kernels, local(): pl.pallas_call(partial(mixer_kernel, H, C, head_dim), out_shape=[jax.Shap...  102 us
    pallas_call x1, Pallas kernels, hand_on(): pl.pallas_call(partial(hand_on_kernel, count), out_shape=[jax.ShapeDtypeS...  5.77 us

profile of v3, /device:TPU:9, one launch (start us, length us, event | category | flops | bytes accessed | tf_op | source)
XLA Modules:
  0.0 108.3 jit_solution(9432387271343991833)
XLA Ops:
  0.6 101.8 %mixer.1 = (bf16[768,2048]{1,0:T(8,128)(2,1)}, bf16[192,8448]{1,0:T(8,128)(2,1)}, f32[32,768]{1,0:T(8,128)}, f32[32,768]{1,0:T(8,128)}) custom-call(bf16[192,8448]{1,0:T(8,128)(2,1)} %cin.1, f32[4,8448]{1,0:T(4,128)} %cw.1, f32[66,128]{1,0:T(8,128)} %bitcast.1, f32[32,768]{1,0:T(8,128)} %step.1, f32[32,768]{1,0:T(8,128)} %rate.1, f32[32]{0:T(128)} %skip.1, ...), custom_call_target="tpu_custom_call" | custom-call | flops 30000001024 | bytes 13000000 | tf_op jit(solution)/shard_map/mixer/pallas_call | solution.py:668
  102.5 5.8 %hand_on.1 = (bf16[768,2048]{1,0:T(8,128)(2,1)}, bf16[192,8448]{1,0:T(8,128)(2,1)}, f32[32,768]{1,0:T(8,128)}, f32[32,768]{1,0:T(8,128)}) custom-call(bf16[768,2048]{1,0:T(8,128)(2,1)} %get-tuple-element.8.refs_0_, bf16[192,8448]{1,0:T(8,128)(2,1)} %get-tuple-element.9.refs_1_, f32[32,768]{1,0:T(8,128)} %get-tuple-element.10.refs_2_, ...), custom_call_target="tpu_custom_call" | custom-call | tf_op jit(solution)/shard_map/hand_on/pallas_call | solution.py:642

commit v4 on v3

--- a/solution.py
+++ b/solution.py
@@ -507,12 +507,20 @@
                 recv_x(k, o).wait_recv()
             states(k)
             chain(1, k)
+
+        @pl.when(k < K - 1)
+        def _():
             intra(k)
             chain(0, k)
 
         @pl.when(k >= 1)
         def _():
             carry_over(k - 1)
+
+        @pl.when(k == K - 1)
+        def _():
+            chain(0, k)
+            intra(k)
 
         @pl.when(k >= 2)
         def _():

time: 108 us -> 108 us (level); the launches traced: 108 us -> 106 us
  Pallas kernels: 108 us -> 106 us
    pallas_call x1, Pallas kernels: 102 us -> 99.9 us  [local(): pl.pallas_call(partial(mixer_kernel, H, C, head_dim), out_shape=[jax.Shap...]
where the time goes in v4:
time: 108 us; the launch traced here: 106 us
  Pallas kernels  106 us (98%)
    pallas_call x1, Pallas kernels, local(): pl.pallas_call(partial(mixer_kernel, H, C, head_dim), out_shape=[jax.Shap...  99.9 us
    pallas_call x1, Pallas kernels, hand_on(): pl.pallas_call(partial(hand_on_kernel, count), out_shape=[jax.ShapeDtypeS...  5.77 us

profile of v4, /device:TPU:9, one launch (start us, length us, event | category | flops | bytes accessed | tf_op | source)
XLA Modules:
  0.0 106.3 jit_solution(10533450706621517036)
XLA Ops:
  0.6 99.9 %mixer.1 = (bf16[768,2048]{1,0:T(8,128)(2,1)}, bf16[192,8448]{1,0:T(8,128)(2,1)}, f32[32,768]{1,0:T(8,128)}, f32[32,768]{1,0:T(8,128)}) custom-call(bf16[192,8448]{1,0:T(8,128)(2,1)} %cin.1, f32[4,8448]{1,0:T(4,128)} %cw.1, f32[66,128]{1,0:T(8,128)} %bitcast.1, f32[32,768]{1,0:T(8,128)} %step.1, f32[32,768]{1,0:T(8,128)} %rate.1, f32[32]{0:T(128)} %skip.1, ...), custom_call_target="tpu_custom_call" | custom-call | flops 30000001024 | bytes 13000000 | tf_op jit(solution)/shard_map/mixer/pallas_call | solution.py:676
  100.6 5.8 %hand_on.1 = (bf16[768,2048]{1,0:T(8,128)(2,1)}, bf16[192,8448]{1,0:T(8,128)(2,1)}, f32[32,768]{1,0:T(8,128)}, f32[32,768]{1,0:T(8,128)}) custom-call(bf16[768,2048]{1,0:T(8,128)(2,1)} %get-tuple-element.8.refs_0_, bf16[192,8448]{1,0:T(8,128)(2,1)} %get-tuple-element.9.refs_1_, f32[32,768]{1,0:T(8,128)} %get-tuple-element.10.refs_2_, ...), custom_call_target="tpu_custom_call" | custom-call | tf_op jit(solution)/shard_map/hand_on/pallas_call | solution.py:650
